TPU v7x, 128 devices: a whole 4x4x4 slice. The times are simulated.
128 devices in a mesh: blk: 16 (over x_lo, z, core), grp: 8 (over y, x_hi).
Axes of the slice: x: 4 (x_hi: 2, x_lo: 2; x = x_hi * 2 + x_lo), y: 4, z: 4, core: 2. Of those that a mesh axis runs over, the one named last changes fastest.
Arguments:
- block_values: bfloat16 [6144, 16, 64, 64], P('blk', 'grp'), may hold values from -1.5 to 1.5
- block_columns: int32 [6144, 16], P('blk', 'grp'), may hold values from 0 to 6143, as said below
- row_counts: int32 [6144], P('blk'), may hold values from 6 to 16
- prolong_blocks: bfloat16 [6144, 64, 64], P(('blk', 'grp')), may hold values from -0.75 to 0.75
- aggregates: int32 [6144], P(('blk', 'grp')), may hold values from 0 to 63, as said below
Outputs:
- coarse_blocks: float32 [64, 64, 64, 64], P('grp', 'blk')
Inputs may be any that keep to these rules, and one draw needn't show every extreme that they name: `aggregates`: the aggregate of a fine block row of panel p, rows p * 384 to (p + 1) * 384 - 1, lies in p * 4 to (p + 1) * 4 - 1. `block_columns`: A block column of a row of panel p lies in a panel p + d modulo the number of panels, for some d of -2 to 2; slot 0 of each row holds the row itself.
All inputs are finite; a program needn't handle non-finite values.
Results may differ from a plain program's by a relative error of at most 0.0029.
Values may be sent and summed in bfloat16 or wider, within the bound.
A program may use at most 192 MiB of HBM per device.

v0:
```python
import jax
import jax.numpy as jnp
from jax import lax
from jax.sharding import Mesh
from jax.sharding import PartitionSpec as P

CB = 4
GRP = ("grp_0", "grp_1")
BLK_GRP = ("blk", "grp_0", "grp_1")


def whole_of(value, axes, dim):
    for axis in reversed(axes):
        value = lax.all_gather(value, axis, axis=dim, tiled=True)
    return value


def passed_along(block, axis, distance):
    devices = range(lax.axis_size(axis))
    route = [((i - distance) % len(devices), i) for i in devices]
    return lax.ppermute(block, axis, route)


def cut_along(value, dim, devices):
    before, after = (value.shape[:dim], value.shape[dim + 1 :])
    return jnp.moveaxis(value.reshape(*before, devices, -1, *after), dim, 0)


def sent_and_summed(value, axis, dim):
    devices = lax.axis_size(axis)
    parts = lax.all_to_all(cut_along(value, dim, devices), axis, 0, 0, tiled=True)
    return jnp.sum(parts, axis=0)


def local(block_values, block_columns, row_counts, prolong_blocks, aggregates):
    panel_length = row_counts.shape[0]
    slots_here = block_values.shape[1]
    slot_total = panel_length * slots_here
    block_size = block_values.shape[2]
    group_size = lax.axis_size(GRP)
    panel_total = lax.axis_size("blk")
    coarse_count = CB * panel_total
    panel_blocks, panel_aggs = (whole_of(prolong_blocks, GRP, 0), whole_of(aggregates, GRP, 0))
    lower = []
    upper = []
    going_down = (panel_blocks, panel_aggs)
    going_up = (panel_blocks, panel_aggs)
    for hop in range(2):
        going_down = passed_along((going_down[0], going_down[1]), "blk", 1)
        lower.insert(0, going_down)
        going_up = passed_along((going_up[0], going_up[1]), "blk", -1)
        upper.append(going_up)
    pieces = lower + [(panel_blocks, panel_aggs)] + upper
    window_blocks = jnp.concatenate([piece[0] for piece in pieces], axis=0)
    window_aggs = jnp.concatenate([piece[1] for piece in pieces], axis=0)
    own_blocks = window_blocks[2 * panel_length : 3 * panel_length]
    own_aggs = window_aggs[2 * panel_length : 3 * panel_length]
    wanted = block_columns.reshape(slot_total)
    column_panel = wanted // panel_length
    distance = jnp.mod(column_panel - lax.axis_index("blk") + 2, panel_total)
    local_rows = distance * panel_length + wanted % panel_length
    fetched = jnp.take(window_blocks, local_rows, axis=0)
    fetched_aggs = jnp.take(window_aggs, local_rows, axis=0)
    prolong_picked = fetched.reshape(panel_length, slots_here, block_size, block_size)
    product = jnp.einsum(
        "rkab,rkbc->rkac", block_values, prolong_picked, preferred_element_type=jnp.float32
    )
    slot_ids = lax.axis_index(GRP) * slots_here + jnp.arange(slots_here, dtype=jnp.int32)
    live = slot_ids[None, :] < row_counts[:, None]
    product = jnp.where(live[:, :, None, None], product, 0.0).astype(jnp.bfloat16)
    restricted = jnp.einsum(
        "rba,rkbc->rkac", own_blocks, product, preferred_element_type=jnp.float32
    ).reshape(slot_total, block_size, block_size)
    local_coarse = own_aggs - lax.axis_index("blk") * CB
    target = fetched_aggs * CB + jnp.broadcast_to(
        local_coarse[:, None], (panel_length, slots_here)
    ).reshape(slot_total)
    share = coarse_count // group_size
    wanted_targets = jnp.arange(share * lax.axis_size(GRP) * CB, dtype=jnp.int32)
    selector = (wanted_targets[:, None] == target[None, :]).astype(jnp.float32)
    summed = jnp.einsum(
        "ts,sab->tab",
        selector,
        restricted,
        precision=lax.Precision.HIGHEST,
        preferred_element_type=jnp.float32,
    )
    return sent_and_summed(
        summed.reshape(share * lax.axis_size(GRP), CB, block_size, block_size), GRP, 0
    )


def solution(mesh):
    finer = Mesh(mesh.devices.reshape(mesh.shape["blk"], 4, 2), ("blk", "grp_0", "grp_1"))
    in_specs = (
        P("blk", GRP, None, None),
        P("blk", GRP),
        P("blk"),
        P(BLK_GRP, None, None),
        P(BLK_GRP),
    )
    out_specs = P(GRP, "blk", None, None)
    return jax.shard_map(local, mesh=finer, in_specs=in_specs, out_specs=out_specs, check_vma=False)
```

profile of v0, /device:TPU:0, one launch (start us, length us, event | category | flops | bytes accessed | tf_op | source)
XLA Modules:
  0.0 503.6 jit_solution(4535315488690570321)
XLA Ops:
  6.6 28.5 %all_gather.14 = bf16[96,64,64]{2,1,0:T(8,128)(2,1)} all-gather(bf16[48,64,64]{2,1,0:T(8,128)(2,1)} %param.8), channel_id=1, replica_groups=mesh['blk'=16,'grp_0'=4,'grp_1'=2] {'grp_1'}, dimensions={0}, use_global_device_ids=true | all-gather | bytes 1179648 | tf_op jit(solution)/shard_map/all_gather | solution.py:14
  35.1 66.4 %all-gather.2.cloned.1.call-done = bf16[384,64,64]{2,1,0:T(8,128)(2,1)} async-done(((bf16[96,64,64]{2,1,0:T(8,128)(2,1)}), bf16[384,64,64]{2,1,0:T(8,128)(2,1)}) %all-gather.2.cloned.1.call-update) | async-done | bytes 3145744 | tf_op jit(solution)/shard_map/all_gather | solution.py:14
  101.5 8.1 %copy.23 = bf16[384,64,64]{0,2,1:T(8,128)(2,1)S(1)} copy(bf16[384,64,64]{2,1,0:T(8,128)(2,1)} %all-gather.2.cloned.1.call-done) | data formatting | bytes 6291456 | tf_op jit(solution)/shard_map/all_gather | solution.py:14
  113.5 35.1 %collective-permute-done.4 = bf16[384,64,64]{0,2,1:T(8,128)(2,1)} collective-permute-done((bf16[384,64,64]{0,2,1:T(8,128)(2,1)S(1)}, bf16[384,64,64]{0,2,1:T(8,128)(2,1)}, u32[]{:S(2)}, u32[]{:S(2)}) %collective-permute-start.4) | collective-permute-done | bytes 3145760 | tf_op jit(solution)/shard_map/ppermute | solution.py:21
  155.1 35.8 %all-reduce = s32[96]{0:T(128)S(1)} all-reduce(s32[96]{0:T(128)S(1)} %dynamic-update-slice), channel_id=1, replica_groups=mesh['blk'=16,'grp_0'=4,'grp_1'=2] {'grp_1'}, use_global_device_ids=true, to_apply=%add | all-reduce | flops 96 | bytes 768
  191.1 8.2 %all-reduce.1 = s32[384]{0:T(512)S(1)} all-reduce(s32[384]{0:T(512)S(1)} %dynamic-update-slice.1), channel_id=1, replica_groups=mesh['blk'=16,'grp_0'=4,'grp_1'=2] {'grp_0'}, use_global_device_ids=true, to_apply=%add.1 | all-reduce | flops 384 | bytes 3072
  205.2 18.5 %copy.30 = bf16[384,2,64,64]{3,2,1,0:T(8,128)(2,1)} copy(bf16[384,2,64,64]{0,3,2,1:T(8,128)(2,1)} %param.5) | data formatting | bytes 12582912 | tf_op args[0]
  228.8 4.6 gather_fusion
  233.4 10.2 %copy.26 = bf16[384,64,64]{2,1,0:T(8,128)(2,1)} copy(bf16[384,64,64]{0,2,1:T(8,128)(2,1)} %collective-permute-done.4) | data formatting | bytes 6291456 | tf_op jit(solution)/shard_map/ppermute | solution.py:21
  243.6 10.2 %copy.27 = bf16[384,64,64]{2,1,0:T(8,128)(2,1)} copy(bf16[384,64,64]{0,2,1:T(8,128)(2,1)} %collective-permute-done.6) | data formatting | bytes 6291456 | tf_op jit(solution)/shard_map/ppermute | solution.py:21
  253.9 10.3 %copy.25 = bf16[384,64,64]{2,1,0:T(8,128)(2,1)} copy(bf16[384,64,64]{0,2,1:T(8,128)(2,1)} %collective-permute-done.5) | data formatting | bytes 6291456 | tf_op jit(solution)/shard_map/ppermute | solution.py:21
  264.2 7.2 %constant_dynamic-update-slice_fusion.5 = bf16[1920,64,64]{2,1,0:T(8,128)(2,1)} fusion(bf16[384,64,64]{2,1,0:T(8,128)(2,1)} %copy.25), kind=kLoop, calls=%fused_computation.27 | loop fusion | bytes 9437184
  283.9 10.4 %copy.28 = bf16[384,64,64]{2,1,0:T(8,128)(2,1)} copy(bf16[384,64,64]{0,2,1:T(8,128)(2,1)} %collective-permute-done.7) | data formatting | bytes 6291456 | tf_op jit(solution)/shard_map/ppermute | solution.py:21
  294.3 7.0 %constant_dynamic-update-slice_fusion.1 = bf16[1920,64,64]{2,1,0:T(8,128)(2,1)} fusion(bf16[1920,64,64]{2,1,0:T(8,128)(2,1)} %constant_dynamic-update-slice_fusion.2, bf16[384,64,64]{2,1,0:T(8,128)(2,1)} %copy.28), kind=kLoop, calls=%fused_computation.23 | loop fusion | bytes 12582912 | tf_op jit(solution)/shard_map/concatenate | solution.py:54
  301.3 29.6 %gather_fusion.1 = bf16[768,64,64]{2,1,0:T(8,128)(2,1)} fusion(bf16[1920,64,64]{2,1,0:T(8,128)(2,1)} %constant_dynamic-update-slice_fusion.1, s32[1024]{0:T(1024)S(1)} %pad_clamp_fusion), kind=kCustom, calls=%fused_computation.1 | custom fusion | bytes 12585984 | tf_op jit(solution)/shard_map/jit(_take)/gather | solution.py:62
  330.9 16.7 %copy.29 = bf16[384,2,64,64]{2,3,1,0:T(8,128)(2,1)} copy(bf16[384,2,64,64]{3,2,1,0:T(8,128)(2,1)} %bitcast.32) | data formatting | bytes 12582912 | tf_op jit(solution)/shard_map/jit(_take)/gather | solution.py:62
  347.5 22.0 %fusion.1 = f32[384,2,64,64]{3,2,1,0:T(8,128)} fusion(pred[384,2]{1,0:T(8,128)(4,1)S(1)} %broadcast_compare_fusion, bf16[384,2,64,64]{3,2,1,0:T(8,128)(2,1)} %copy.30, bf16[384,2,64,64]{2,3,1,0:T(8,128)(2,1)} %copy.29, pred[384,2]{1,0:T(8,128)(4,1)S(1)} %copy.22, bf16[384,64,64]{2,1,0:T(8,128)(2,1)} %all-gather.2.cloned.1.call-done), kind=kOutput, calls=%fused_computation.4 | convolution fusion | flops 814743552 | bytes 28313088 | tf_op jit(solution)/shard_map/rba,rkbc->rkac/dot_general | solution.py:71
  369.5 22.6 %copy.35 = f32[768,64,64,1,1]{0,2,1,4,3:T(8,128)} copy(f32[768,64,64,1,1]{1,2,0,4,3:T(8,128)} %bitcast.29) | data formatting | bytes 25165824 | tf_op jit(solution)/shard_map/reshape | solution.py:73
  392.1 14.1 %fusion.37 = f32[8,4,64,8,64]{4,3,2,1,0:T(8,128)} fusion(f32[768,64,64,1,1]{0,2,1,4,3:T(8,128)} %copy.35, s32[768]{0:T(1024)S(1)} %multiply_add_fusion.1, s32[8,8,4]{1,2,0:T(4,128)S(1)} %multiply_add_fusion), kind=kOutput, calls=%fused_computation.72 | convolution fusion | flops 9663873024 | bytes 16781312 | tf_op jit(solution)/shard_map/ts,sab->tab/dot_general | solution.py:81
  406.2 9.8 %reshape.278 = f32[8,1,131072]{2,1,0:T(1,128)} reshape(f32[8,4,64,8,64]{4,3,2,1,0:T(8,128)} %fusion.37) | data formatting | bytes 8388608
  416.0 52.0 %all_to_all.5 = f32[8,1,131072]{2,1,0:T(1,128)} all-to-all(f32[8,1,131072]{2,1,0:T(1,128)} %reshape.278), channel_id=1, replica_groups=mesh['blk'=16,'grp_0'=4,'grp_1'=2] {'grp_0','grp_1'}, dimensions={0} | all-to-all | bytes 8388608 | tf_op jit(solution)/shard_map/all_to_all | solution.py:31
  468.5 13.7 %reduce.2 = f32[8,131072]{1,0:T(8,128)} reduce(f32[8,1,131072]{2,1,0:T(1,128)} %all_to_all.5, f32[]{:T(128)} %broadcast.346), dimensions={1}, to_apply=%all_to_all.3.reduce_sub_computation | reduce | bytes 8388612 | tf_op jit(solution)/shard_map/all_to_all | solution.py:31
  482.2 8.7 %reshape.279 = f32[8,4,64,8,64]{4,3,2,1,0:T(8,128)} reshape(f32[8,131072]{1,0:T(8,128)} %reduce.2) | data formatting | bytes 8388608
  490.9 4.3 bitcast_reduce_fusion
  (79 shorter events, 34.5 us)
Async XLA Ops:
  6.5 145.9 %copy-start.4 = (u32[128]{0:T(128)S(1)}, u32[128]{0:T(128)}, u32[]{:S(2)}) copy-start(u32[128]{0:T(128)} %constant.94) | copy-start | bytes 1540
  6.5 146.5 %copy-start.3 = (u32[128]{0:T(128)S(1)}, u32[128]{0:T(128)}, u32[]{:S(2)}) copy-start(u32[128]{0:T(128)} %constant.99) | copy-start | bytes 1540
  6.5 148.4 %copy-start.2 = (s32[48]{0:T(128)S(1)}, s32[48]{0:T(128)}, u32[]{:S(2)}) copy-start(s32[48]{0:T(128)} %param.9) | copy-start | bytes 580
  6.5 196.6 %copy-start = (s32[384,2]{0,1:T(2,128)S(1)}, s32[384,2]{0,1:T(2,128)}, u32[]{:S(2)}) copy-start(s32[384,2]{0,1:T(2,128)} %param.6) | copy-start | bytes 9220
  6.5 197.7 %copy-start.1 = (s32[384]{0:T(512)S(1)}, s32[384]{0:T(512)}, u32[]{:S(2)}) copy-start(s32[384]{0:T(512)} %param.7) | copy-start | bytes 4612
  6.5 94.9 %all-gather.2.cloned.1.call-start = ((), (), s32[]{:S(2)}) async-start(), calls=%async_computation.1 | async-start | bytes 7864320 | tf_op jit(solution)/shard_map/all_gather | solution.py:14
  109.6 39.0 %collective-permute-start.4 = (bf16[384,64,64]{0,2,1:T(8,128)(2,1)S(1)}, bf16[384,64,64]{0,2,1:T(8,128)(2,1)}, u32[]{:S(2)}, u32[]{:S(2)}) collective-permute-start(bf16[384,64,64]{0,2,1:T(8,128)(2,1)S(1)} %copy.23), channel_id=1, source_target_pairs={{120,0},{0,8},{8,16},{16,24},{24,32},{32,40},{40,48},{48,56},{56,6... | collective-permute-start | bytes 9437192 | tf_op jit(solution)/shard_map/ppermute | solution.py:21
  109.7 38.9 %collective-permute-start.6 = (bf16[384,64,64]{0,2,1:T(8,128)(2,1)S(1)}, bf16[384,64,64]{0,2,1:T(8,128)(2,1)}, u32[]{:S(2)}, u32[]{:S(2)}) collective-permute-start(bf16[384,64,64]{0,2,1:T(8,128)(2,1)S(1)} %copy.23), channel_id=1, source_target_pairs={{8,0},{16,8},{24,16},{32,24},{40,32},{48,40},{56,48},{64,56},{72,6... | collective-permute-start | bytes 9437192 | tf_op jit(solution)/shard_map/ppermute | solution.py:21
  148.6 105.3 %collective-permute-start.5 = (bf16[384,64,64]{0,2,1:T(8,128)(2,1)}, bf16[384,64,64]{0,2,1:T(8,128)(2,1)}, u32[]{:S(2)}, u32[]{:S(2)}) collective-permute-start(bf16[384,64,64]{0,2,1:T(8,128)(2,1)} %collective-permute-done.4), channel_id=1, source_target_pairs={{120,0},{0,8},{8,16},{16,24},{24,32},{32,40},{40,48},{48,56},{56,6... | collective-permute-start | bytes 9437192 | tf_op jit(solution)/shard_map/ppermute | solution.py:21
  148.6 135.3 %collective-permute-start.7 = (bf16[384,64,64]{0,2,1:T(8,128)(2,1)}, bf16[384,64,64]{0,2,1:T(8,128)(2,1)}, u32[]{:S(2)}, u32[]{:S(2)}) collective-permute-start(bf16[384,64,64]{0,2,1:T(8,128)(2,1)} %collective-permute-done.6), channel_id=1, source_target_pairs={{8,0},{16,8},{24,16},{32,24},{40,32},{48,40},{56,48},{64,56},{72,6... | collective-permute-start | bytes 9437192 | tf_op jit(solution)/shard_map/ppermute | solution.py:21
  199.3 5.1 %collective-permute-start = (s32[384]{0:T(512)S(1)}, s32[384]{0:T(512)S(1)}, u32[]{:S(2)}, u32[]{:S(2)}) collective-permute-start(s32[384]{0:T(512)S(1)} %all-reduce.1), channel_id=1, source_target_pairs={{120,0},{0,8},{8,16},{16,24},{24,32},{32,40},{40,48},{48,56},{56,6... | collective-permute-start | bytes 4616 | tf_op jit(solution)/shard_map/ppermute | solution.py:21
  199.3 24.3 %collective-permute-start.2 = (s32[384]{0:T(512)S(1)}, s32[384]{0:T(512)S(1)}, u32[]{:S(2)}, u32[]{:S(2)}) collective-permute-start(s32[384]{0:T(512)S(1)} %all-reduce.1), channel_id=1, source_target_pairs={{8,0},{16,8},{24,16},{32,24},{40,32},{48,40},{56,48},{64,56},{72,6... | collective-permute-start | bytes 4616 | tf_op jit(solution)/shard_map/ppermute | solution.py:21
  204.4 23.0 %collective-permute-start.1 = (s32[384]{0:T(512)S(1)}, s32[384]{0:T(512)S(1)}, u32[]{:S(2)}, u32[]{:S(2)}) collective-permute-start(s32[384]{0:T(512)S(1)} %collective-permute-done), channel_id=1, source_target_pairs={{120,0},{0,8},{8,16},{16,24},{24,32},{32,40},{40,48},{48,56},{56,6... | collective-permute-start | bytes 4616 | tf_op jit(solution)/shard_map/ppermute | solution.py:21
  223.7 5.1 %collective-permute-start.3 = (s32[384]{0:T(512)S(1)}, s32[384]{0:T(512)S(1)}, u32[]{:S(2)}, u32[]{:S(2)}) collective-permute-start(s32[384]{0:T(512)S(1)} %collective-permute-done.2), channel_id=1, source_target_pairs={{8,0},{16,8},{24,16},{32,24},{40,32},{48,40},{56,48},{64,56},{72,6... | collective-permute-start | bytes 4616 | tf_op jit(solution)/shard_map/ppermute | solution.py:21
  253.9 17.5 %slice-start.4 = ((s8[6291456]{0:T(1024)(128)(4,1)}), s8[2097152]{0:T(1024)(128)(4,1)S(1)}, s32[]{:S(2)}) async-start(s8[6291456]{0:T(1024)(128)(4,1)} %bitcast.35), calls=%async_computation.6 | async-start | bytes 4194304
  264.2 7.2 %slice-start.5 = ((s8[6291456]{0:T(1024)(128)(4,1)}), s8[4194304]{0:T(1024)(128)(4,1)S(1)}, s32[]{:S(2)}) async-start(s8[6291456]{0:T(1024)(128)(4,1)} %bitcast.35), calls=%async_computation.7 | async-start | bytes 8388608
  264.2 11.4 %slice-start = ((s8[6291456]{0:T(1024)(128)(4,1)}), s8[4194304]{0:T(1024)(128)(4,1)S(1)}, s32[]{:S(2)}) async-start(s8[6291456]{0:T(1024)(128)(4,1)} %bitcast.30), calls=%async_computation.2 | async-start | bytes 8388608
  271.4 4.2 slice-start.1
  271.4 8.4 %slice-start.2 = ((s8[6291456]{0:T(1024)(128)(4,1)}), s8[4194304]{0:T(1024)(128)(4,1)S(1)}, s32[]{:S(2)}) async-start(s8[6291456]{0:T(1024)(128)(4,1)} %bitcast.33), calls=%async_computation.4 | async-start | bytes 8388608
  275.7 4.1 slice-start.3
Sparse Core Ops, SparseCore 0:
  35.2 66.2 all-gather.1
where the time goes:
time: 512 us; the launch traced here: 504 us
  local copies, waits for them, and re-layouts  191 us (37%)
  blocking collectives  125 us (24%)
  waiting for transfers between devices  102 us (20%)
  matrix products  36.1 us (7%)
  other arithmetic  18.2 us (4%)
  starting transfers between devices  15.6 us (3%)
  between operations  15.3 us (3%)
    all_gather x1, waiting for transfers between devices, whole_of(): value = lax.all_gather(value, axis, axis=dim, tiled=True)  66.4 us
    unnamed x38, local copies, waits for them, and re-layouts  58.3 us
    all_to_all x1, blocking collectives, sent_and_summed(): lax.all_to_all(cut_along(value, dim, devices), axis, 0, 0, tiled=True)  52 us
    gather x2, local copies, waits for them, and re-layouts, local(): fetched = jnp.take(window_blocks, local_rows, axis=0)  46.2 us
    unnamed x2, blocking collectives  44 us
    ppermute x4, local copies, waits for them, and re-layouts, passed_along(): return lax.ppermute(block, axis, route)  41.2 us
    ppermute x8, waiting for transfers between devices, passed_along(): return lax.ppermute(block, axis, route)  36.1 us
    all_gather x1, blocking collectives, whole_of(): value = lax.all_gather(value, axis, axis=dim, tiled=True)  28.5 us
  transfers between devices with their start and end apart: 9, of which 3 were waited for; matrix products, arithmetic and copies ran while one was open for 15% of the time, Pallas kernels for 0%

commit v1 on v0

v1 whole, which is shorter than its diff:
```python
import functools

import jax
import jax.numpy as jnp
from jax import lax
from jax.experimental import pallas as pl
from jax.experimental.pallas import tpu as pltpu
from jax.sharding import PartitionSpec as P

MESH = pl.DeviceIdType.MESH
BF16, F32 = jnp.bfloat16, jnp.float32

BS = 64
CB = 4
ROWS = 384
SHARD = 48
PAIRS = SHARD // 2
PANELS = 16
GROUP = 8
SPAN = 5
HEAD = 16
LEN = HEAD + PAIRS * BS
CUT = HEAD + 14 * BS
F_PART, L_PART = (0, CUT), (CUT, LEN - CUT)
F_HALVES = ((0, 448), (448, CUT - 448))
L_HALVES = ((CUT, 320), (CUT + 320, 320))
SLOTS = 2
TARGETS = SPAN * CB * CB * 2
ACCS = TARGETS + 8
BLOCKS = TARGETS // 4
SHARE = BLOCKS // GROUP


def gather_kernel(p_ref, agg_ref, win_ref, raw, own, local_sem, send_sem, recv_sem):
    b, g = lax.axis_index("blk"), lax.axis_index("grp")
    core = b % 2
    y, h = g // 2, g % 2
    up_k, down_k = ((b + 2) % PANELS, g), ((b + PANELS - 2) % PANELS, g)
    up_y, down_y = (b, (g + 2) % GROUP), (b, (g + GROUP - 2) % GROUP)
    across, sibling = (b, g + 1 - 2 * h), (b + 1 - 2 * core, g)

    load = pltpu.make_async_copy(p_ref, raw, local_sem.at[0])
    load.start()
    barrier = pltpu.get_barrier_semaphore()
    for device in (up_k, down_k, up_y, down_y, across, sibling):
        pl.semaphore_signal(barrier, inc=1, device_id=device, device_id_type=MESH)
    load.wait()
    own[0:HEAD, :] = agg_ref[...]

    def pack(j, carry):
        row = pl.multiple_of(HEAD + j * BS, HEAD)
        own[pl.ds(row, BS), :] = jnp.concatenate([raw[2 * j], raw[2 * j + 1]], axis=-1)
        return carry

    lax.fori_loop(0, PAIRS, pack, 0)
    keep = pltpu.make_async_copy(own, win_ref.at[2, g], local_sem.at[1])
    keep.start()
    pl.semaphore_wait(barrier, 6)

    copies = {}

    def at(d, dy, dh):
        return win_ref.at[d, ((y + dy) % 4) * 2 + (h + dh) % 2]

    def send(name, part, d, dy, dh, to_d, device, src=None):
        start, size = part
        piece = pl.ds(start, size)
        n = len(copies)
        source = own if src is not None else at(d, dy, dh)
        copies[name] = pltpu.make_async_remote_copy(
            src_ref=source.at[piece, :],
            dst_ref=at(to_d, dy, dh).at[piece, :],
            send_sem=send_sem.at[n],
            recv_sem=recv_sem.at[n],
            device_id=device,
            device_id_type=MESH,
        )
        copies[name].start()

    def got(*names):
        for name in names:
            copies[name].wait_recv()

    def to_y(part, tag, d, dh, src=None):
        send((tag, "y+", d, dh), part, d, 0, dh, d, up_y, src)
        send((tag, "y-", d, dh), part, d, 0, dh, d, down_y, src)

    def on_y(halves, tag, d, dh):
        send((tag, "f+", d, dh), halves[0], d, -1, dh, d, up_y)
        send((tag, "f-", d, dh), halves[1], d, 1, dh, d, down_y)

    def to_z(part, tag, dy, dh, src=None):
        send((tag, "z+", dy, dh), part, 2, dy, dh, 0, up_k, src)
        send((tag, "z-", dy, dh), part, 2, dy, dh, 4, down_k, src)

    def over(part, tag, dy, dh, src=None):
        send((tag, "s", dy, dh), part, 2, dy, dh, 1 + 2 * core, sibling, src)

    def over_far(part, tag, dy, dh):
        send((tag, "t", dy, dh), part, 4 - 4 * core, dy, dh, 3 - 2 * core, sibling)

    send(("F", "x"), F_PART, 2, 0, 0, 2, across, own)
    to_y(F_PART, "F", 2, 0, own)
    to_z(F_PART, "F", 0, 0, own)
    send(("L", "x"), L_PART, 2, 0, 0, 2, across, own)
    to_z(L_PART, "L", 0, 0, own)
    to_y(L_PART, "L", 2, 0, own)
    over((0, LEN), "A", 0, 0, own)

    got(("F", "x"))
    to_y(F_PART, "F", 2, 1)
    to_z(F_PART, "F", 0, 1)
    got(("F", "y+", 2, 0), ("F", "y-", 2, 0))
    on_y(F_HALVES, "F", 2, 0)
    for dy in (-1, 1):
        to_z(F_PART, "F", dy, 0)
    got(("L", "x"))
    to_z(L_PART, "L", 0, 1)
    to_y(L_PART, "L", 2, 1)
    over((0, LEN), "A", 0, 1)
    got(("L", "y+", 2, 0), ("L", "y-", 2, 0))
    on_y(L_HALVES, "L", 2, 0)
    for dy in (-1, 1):
        over((0, LEN), "A", dy, 0)
    got(("L", "z+", 0, 0), ("L", "z-", 0, 0))
    for d in (0, 4):
        to_y(L_PART, "L", d, 0)
    over_far(L_PART, "L", 0, 0)
    got(("F", "y+", 2, 1), ("F", "y-", 2, 1))
    on_y(F_HALVES, "F", 2, 1)
    for dy in (-1, 1):
        to_z(F_PART, "F", dy, 1)
    got(("F", "f+", 2, 0), ("F", "f-", 2, 0))
    to_z(F_PART, "F", 2, 0)
    got(("L", "z+", 0, 1), ("L", "z-", 0, 1))
    for d in (0, 4):
        to_y(L_PART, "L", d, 1)
    over_far(L_PART, "L", 0, 1)
    got(("F", "f+", 2, 1), ("F", "f-", 2, 1))
    to_z(F_PART, "F", 2, 1)
    got(("L", "y+", 2, 1), ("L", "y-", 2, 1))
    on_y(L_HALVES, "L", 2, 1)
    for dy in (-1, 1):
        over((0, LEN), "A", dy, 1)
    got(("L", "f+", 2, 0), ("L", "f-", 2, 0))
    over((0, LEN), "A", 2, 0)
    got(("F", "z+", 0, 0), ("F", "z-", 0, 0))
    over_far(F_PART, "F", 0, 0)
    for d in (0, 4):
        got(("L", "y+", d, 0), ("L", "y-", d, 0))
        on_y(L_HALVES, "L", d, 0)
    for dy in (-1, 1):
        over_far(L_PART, "L", dy, 0)
    got(("L", "f+", 2, 1), ("L", "f-", 2, 1))
    over((0, LEN), "A", 2, 1)
    got(("F", "z+", 0, 1), ("F", "z-", 0, 1))
    over_far(F_PART, "F", 0, 1)
    for dy in (-1, 1):
        got(("F", "z+", dy, 0), ("F", "z-", dy, 0))
        over_far(F_PART, "F", dy, 0)
    for d in (0, 4):
        got(("L", "y+", d, 1), ("L", "y-", d, 1))
        on_y(L_HALVES, "L", d, 1)
    for dy in (-1, 1):
        over_far(L_PART, "L", dy, 1)
    for dy, dh in ((-1, 1), (1, 1), (2, 0), (2, 1)):
        got(("F", "z+", dy, dh), ("F", "z-", dy, dh))
        over_far(F_PART, "F", dy, dh)
    for dh in (0, 1):
        for d in (0, 4):
            got(("L", "f+", d, dh), ("L", "f-", d, dh))
        over_far(L_PART, "L", 2, dh)
    for name in copies:
        if name[1] in ("s", "t"):
            got(name)
    for copy in copies.values():
        copy.wait_send()
    keep.wait()


COPIES = 86 - 8


def gathered(prolong, aggs):
    return pl.pallas_call(
        gather_kernel,
        out_shape=jax.ShapeDtypeStruct((SPAN, GROUP, LEN, 2 * BS), BF16),
        in_specs=[
            pl.BlockSpec(memory_space=pl.ANY),
            pl.BlockSpec(memory_space=pltpu.VMEM),
        ],
        out_specs=pl.BlockSpec(memory_space=pl.ANY),
        scratch_shapes=[
            pltpu.VMEM((SHARD, BS, BS), BF16),
            pltpu.VMEM((LEN, 2 * BS), BF16),
            pltpu.SemaphoreType.DMA((2,)),
            pltpu.SemaphoreType.DMA((COPIES,)),
            pltpu.SemaphoreType.DMA((COPIES,)),
        ],
        compiler_params=pltpu.CompilerParams(collective_id=0, has_side_effects=True),
        name="gather_window",
    )(prolong, aggs)


def compute_kernel(
    row_ref, loc_ref, base_ref, tj_ref, a_ref, win_ref, part_ref, turned, blocks, acc
):
    def clear(t, carry):
        acc[t] = jnp.zeros((BS, 2 * BS), F32)
        return carry

    lax.fori_loop(0, ACCS, clear, 0)

    for first in range(0, ROWS, 128):

        def turn(r, carry, first=first):
            both = jnp.concatenate(
                [a_ref[s, r, :, first : first + 128] for s in range(SLOTS)], axis=0
            )
            turned[pl.ds(pl.multiple_of(r * 128, 128), 128), :] = both.astype(F32).T
            return carry

        lax.fori_loop(0, BS, turn, 0, unroll=4)

        def collect(i, carry, first=first):
            blocks[first + i] = turned[pl.ds(i, BS, stride=128), :].astype(BF16)
            return carry

        lax.fori_loop(0, 128, collect, 0, unroll=8)

    for shard in range(GROUP):

        def left(j, carry, shard=shard):
            start = (2 * GROUP + shard) * LEN + HEAD + j * BS
            both = win_ref[pl.ds(pl.multiple_of(start, HEAD), BS), :].T
            for half in range(2):
                i = shard * SHARD + 2 * j + half
                t = jnp.dot(
                    both[half * BS : (half + 1) * BS, :],
                    blocks[i],
                    preferred_element_type=F32,
                )
                blocks[i] = t.astype(BF16)
            return carry

        lax.fori_loop(0, PAIRS, left, 0, unroll=4)

    def right(i, carry):
        t = blocks[i]
        none = jnp.zeros((BS, 2 * BS), BF16)
        for s in range(SLOTS):
            row = pl.multiple_of(row_ref[s, i], HEAD)
            picked = win_ref[pl.ds(row, BS), :]
            stack = [picked, none] if s == 0 else [none, picked]
            r = jnp.dot(t, jnp.concatenate(stack, axis=0), preferred_element_type=F32)
            target = tj_ref[loc_ref[s, i]] + base_ref[s, i]
            acc[target] += r
        return carry

    lax.fori_loop(0, ROWS, right, 0, unroll=4)

    low = lax.broadcasted_iota(jnp.int32, (BS, 2 * BS), 1) < BS

    def fold(t, carry):
        one, two = acc[4 * t], acc[4 * t + 1]
        three, four = acc[4 * t + 2], acc[4 * t + 3]
        first = one + pltpu.roll(two, BS, 1)
        second = pltpu.roll(three, BS, 1) + four
        part_ref[t] = jnp.where(low, first, second)
        return carry

    lax.fori_loop(0, BLOCKS, fold, 0)


def computed(rows, locs, bases, tj, a, win):
    smem = pl.BlockSpec(memory_space=pltpu.SMEM)
    vmem = pl.BlockSpec(memory_space=pltpu.VMEM)
    return pl.pallas_call(
        compute_kernel,
        out_shape=jax.ShapeDtypeStruct((BLOCKS, BS, 2 * BS), F32),
        in_specs=[smem, smem, smem, smem, vmem, vmem],
        out_specs=vmem,
        scratch_shapes=[
            pltpu.VMEM((BS * 128, 128), F32),
            pltpu.VMEM((ROWS, BS, 2 * BS), BF16),
            pltpu.VMEM((ACCS, BS, 2 * BS), F32),
        ],
        compiler_params=pltpu.CompilerParams(vmem_limit_bytes=56 * 2**20),
        name="triple_products",
    )(rows, locs, bases, tj, a, win)


def reduce_kernel(part_ref, out_ref, landed, total, placed, send_sem, recv_sem, send2, recv2):
    b, g = lax.axis_index("blk"), lax.axis_index("grp")
    others = [(g + n) % GROUP for n in range(1, GROUP)]
    barrier = pltpu.get_barrier_semaphore()
    for other in others:
        pl.semaphore_signal(barrier, inc=1, device_id=(b, other), device_id_type=MESH)
    pl.semaphore_wait(barrier, GROUP - 1)
    first = []
    for n, other in enumerate(others):
        copy = pltpu.make_async_remote_copy(
            src_ref=part_ref.at[pl.ds(other * SHARE, SHARE)],
            dst_ref=landed.at[n],
            send_sem=send_sem.at[n],
            recv_sem=recv_sem.at[n],
            device_id=(b, other),
            device_id_type=MESH,
        )
        copy.start()
        first.append(copy)
    out_ref[...] = jnp.zeros(out_ref.shape, F32)
    total[...] = part_ref[pl.ds(g * SHARE, SHARE)]
    for n, copy in enumerate(first):
        copy.wait_recv()
        total[...] += landed[n]

    def owner(m):
        panel = (b + PANELS - 2 + m // 8) % PANELS
        return panel, panel // 2

    def hop(e, m, device):
        return pltpu.make_async_remote_copy(
            src_ref=total.at[e],
            dst_ref=placed.at[m],
            send_sem=send2.at[e],
            recv_sem=recv2.at[m],
            device_id=(b, device),
            device_id_type=MESH,
        )

    def keep(panel, m, block):
        row = (panel % 2) * CB + (m % 8) // 2
        column = (m % 2) * 2
        out_ref[row, column] = block[:, :BS]
        out_ref[row, column + 1] = block[:, BS:]

    for e in range(SHARE):
        m = g * SHARE + e
        panel, device = owner(m)

        @pl.when(device != g)
        def _(e=e, m=m, device=device):
            hop(e, m, device).start()

        @pl.when(device == g)
        def _(e=e, m=m, panel=panel):
            keep(panel, m, total[e])

    def arrive(m, carry):
        panel, device = owner(m)

        @pl.when(jnp.logical_and(device == g, m // SHARE != g))
        def _():
            hop(0, m, (g + 1) % GROUP).wait_recv()
            keep(panel, m, placed[m])

        return carry

    lax.fori_loop(0, BLOCKS, arrive, 0)
    for e in range(SHARE):
        m = g * SHARE + e
        panel, device = owner(m)

        @pl.when(device != g)
        def _(e=e, m=m, device=device):
            hop(e, m, device).wait_send()

    for copy in first:
        copy.wait_send()


def reduced(part):
    vmem = pl.BlockSpec(memory_space=pltpu.VMEM)
    return pl.pallas_call(
        reduce_kernel,
        out_shape=jax.ShapeDtypeStruct((GROUP, CB, BS, BS), F32),
        in_specs=[vmem],
        out_specs=vmem,
        scratch_shapes=[
            pltpu.VMEM((GROUP - 1, SHARE, BS, 2 * BS), F32),
            pltpu.VMEM((SHARE, BS, 2 * BS), F32),
            pltpu.VMEM((BLOCKS, BS, 2 * BS), F32),
            pltpu.SemaphoreType.DMA((GROUP - 1,)),
            pltpu.SemaphoreType.DMA((GROUP - 1,)),
            pltpu.SemaphoreType.DMA((SHARE,)),
            pltpu.SemaphoreType.DMA((BLOCKS,)),
        ],
        compiler_params=pltpu.CompilerParams(collective_id=1, has_side_effects=True),
        name="reduce_blocks",
    )(part)


def local(block_values, block_columns, row_counts, prolong_blocks, aggregates):
    b, g = lax.axis_index("blk"), lax.axis_index("grp")
    head = jnp.pad((aggregates % CB).astype(BF16)[None, :], ((0, HEAD - 1), (0, 2 * BS - SHARD)))
    win = gathered(prolong_blocks, head)

    loc = jnp.mod(block_columns.T - (b - 2) * ROWS, PANELS * ROWS)
    slot = g * SLOTS + jnp.arange(SLOTS, dtype=jnp.int32)
    live = slot[:, None] < row_counts[None, :]
    loc = jnp.where(live, loc, SPAN * ROWS)
    rows = (loc // SHARD) * LEN + HEAD + (loc % SHARD) // 2 * BS
    rows = jnp.where(live, rows, HEAD)

    near = win[:, :, 0, :SHARD].astype(jnp.int32).reshape(SPAN, ROWS)
    tj = (jnp.arange(SPAN, dtype=jnp.int32)[:, None] * CB + near) * (2 * CB)
    tj = jnp.concatenate([tj.reshape(-1), jnp.full((128,), TARGETS, jnp.int32)])
    bases = jnp.where(live, near[2][None, :] * 2 + loc % 2, 0)

    a = jnp.transpose(block_values, (1, 2, 3, 0))
    part = computed(rows, loc, bases, tj, a, win.reshape(-1, 2 * BS))
    return reduced(part)


def solution(mesh):
    in_specs = (
        P("blk", "grp", None, None),
        P("blk", "grp"),
        P("blk"),
        P(("blk", "grp"), None, None),
        P(("blk", "grp")),
    )
    out_specs = P("grp", "blk", None, None)
    return jax.shard_map(local, mesh=mesh, in_specs=in_specs, out_specs=out_specs, check_vma=False)
```

time: 512 us -> 168 us (0.33); the launches traced: 504 us -> 166 us
  local copies, waits for them, and re-layouts: 191 us -> 3.75 us
  Pallas kernels: 0 us -> 158 us
  blocking collectives: 125 us -> 0 us
  waiting for transfers between devices: 102 us -> 0 us
  matrix products: 36.1 us -> 0 us
  starting transfers between devices: 15.6 us -> 0 us
  between operations: 15.3 us -> 0.04 us
  other arithmetic: 18.2 us -> 3.73 us
    pallas_call x0 -> x3, Pallas kernels: none -> 158 us  [the longest x1 68.3 us: gathered(): pl.pallas_call(gather_kernel, out_shape=jax.ShapeDtypeStruct((SPAN, GROUP...]
    all_gather x1 -> x0, waiting for transfers between devices: 66.4 us -> none  [whole_of(): value = lax.all_gather(value, axis, axis=dim, tiled=True)]
    unnamed x38 -> x7, local copies, waits for them, and re-layouts: 58.3 us -> 2.32 us
    all_to_all x1 -> x0, blocking collectives: 52 us -> none  [sent_and_summed(): lax.all_to_all(cut_along(value, dim, devices), axis, 0, 0, tiled=True)]
    gather x3 -> x0, local copies, waits for them, and re-layouts: 50.9 us -> none  [the longest x2 46.2 us: local(): fetched = jnp.take(window_blocks, local_rows, axis=0)]
    unnamed x2 -> x0, blocking collectives: 44 us -> none
    ppermute x4 -> x0, local copies, waits for them, and re-layouts: 41.2 us -> none  [passed_along(): return lax.ppermute(block, axis, route)]
    ppermute x8 -> x0, waiting for transfers between devices: 36.1 us -> none  [passed_along(): return lax.ppermute(block, axis, route)]
  transfers between devices with their start and end apart: 9 -> 0, of which waited for: 3 -> 0; matrix products, arithmetic and copies ran while one was open for 15% -> 0% of each run, Pallas kernels for 0% -> 0%
where the time goes in v1:
time: 168 us; the launch traced here: 166 us
  Pallas kernels  158 us (94%)
  local copies, waits for them, and re-layouts  3.75 us (2%)
  other arithmetic  3.73 us (2%)
    pallas_call x1, Pallas kernels, gathered(): pl.pallas_call(gather_kernel, out_shape=jax.ShapeDtypeStruct((SPAN, GROUP...  68.3 us
    pallas_call x1, Pallas kernels, computed(): pl.pallas_call(compute_kernel, out_shape=jax.ShapeDtypeStruct((BLOCKS, BS...  56 us
    pallas_call x1, Pallas kernels, reduced(): pl.pallas_call(reduce_kernel, out_shape=jax.ShapeDtypeStruct((GROUP, CB,...  33.9 us

profile of v1, /device:TPU:0, one launch (start us, length us, event | category | flops | bytes accessed | tf_op | source)
XLA Modules:
  0.0 165.8 jit_solution(17683926950125321917)
XLA Ops:
  0.0 0.0 copy-start.1
  0.0 0.0 copy-start.2
  0.0 0.7 fusion.3
  0.7 0.6 pad.5.agg_ref
  1.3 0.1 add.76
  1.4 68.3 %gather_window.1 = bf16[5,8,1552,128]{3,2,1,0:T(8,128)(2,1)} custom-call(bf16[48,64,64]{2,1,0:T(8,128)(2,1)} %p_ref.1, bf16[16,128]{1,0:T(8,128)(2,1)} %pad.5.agg_ref), custom_call_target="tpu_custom_call" | custom-call | tf_op jit(solution)/shard_map/gather_window/pallas_call | solution.py:185
  69.7 0.7 multiply_reduce_fusion
  70.4 0.1 mul.56
  70.5 0.0 copy-done.1
  70.5 0.0 copy-done.2
  70.5 0.7 compare_select_fusion
  71.2 0.0 copy-start
  71.2 0.7 compare_select_fusion.1.row_ref
  71.9 1.0 convert_reduce_fusion
  72.8 0.1 reshape.36
  72.9 0.6 concatenate.3.tj_ref
  73.5 0.0 copy-done
  73.5 56.0 %triple_products.1.part_ref = f32[40,64,128]{2,1,0:T(8,128)} custom-call(s32[2,384]{1,0:T(2,128)} %compare_select_fusion.1.row_ref, s32[2,384]{1,0:T(2,128)} %copy-done, s32[2,384]{1,0:T(2,128)} %get-tuple-element.5.base_ref, s32[2048]{0:T(1024)} %concatenate.3.tj_ref, bf16[2,64,64,384]{3,2,1,0:T(8,128)(2,1)} %bitcast.8, bf16[62080,128]{1,0:T(8,128)(2,1)} %bitcast.7), custom_call_target="tpu_custom_call" | custom-call | tf_op jit(solution)/shard_map/triple_products/pallas_call | solution.py:278
  129.5 33.9 %reduce_blocks.1 = f32[8,4,64,64]{3,2,1,0:T(8,128)} custom-call(f32[40,64,128]{2,1,0:T(8,128)} %triple_products.1.part_ref), custom_call_target="tpu_custom_call" | custom-call | tf_op jit(solution)/shard_map/reduce_blocks/pallas_call | solution.py:375
  163.5 2.3 %copy.7 = f32[8,4,64,64]{3,2,1,0:T(8,128)} copy(f32[8,4,64,64]{3,2,1,0:T(8,128)} %reduce_blocks.1) | data formatting | bytes 1048576
  (4 shorter events, 0.0 us)
Async XLA Ops:
  0.0 70.5 %copy-start.1 = (s32[384]{0:T(512)S(1)}, s32[384]{0:T(512)}, u32[]{:S(2)}) copy-start(s32[384]{0:T(512)} %param.7) | copy-start | bytes 4612
  0.0 70.5 %copy-start.2 = (s32[384,2]{0,1:T(2,128)S(1)}, s32[384,2]{0,1:T(2,128)}, u32[]{:S(2)}) copy-start(s32[384,2]{0,1:T(2,128)} %param.6) | copy-start | bytes 9220
  71.2 2.3 %copy-start = (s32[2,384]{1,0:T(2,128)}, s32[2,384]{1,0:T(2,128)S(1)}, u32[]{:S(2)}) copy-start(s32[2,384]{1,0:T(2,128)S(1)} %get-tuple-element.6.loc_ref) | copy-start | bytes 9220

commit v2 on v1

--- a/solution.py
+++ b/solution.py
@@ -29,9 +29,47 @@
 ACCS = TARGETS + 8
 BLOCKS = TARGETS // 4
 SHARE = BLOCKS // GROUP
-
-
-def gather_kernel(p_ref, agg_ref, win_ref, raw, own, local_sem, send_sem, recv_sem):
+PITCH = 136
+
+
+def turn(a_ref, turned, blocks, first):
+    def over(r, carry):
+        both = jnp.concatenate(
+            [a_ref[s, r, :, first : first + 128] for s in range(SLOTS)], axis=0
+        )
+        start = pl.multiple_of(r * PITCH, 8)
+        turned[pl.ds(start, 128), :] = both.T.astype(F32)
+        return carry
+
+    lax.fori_loop(0, BS, over, 0, unroll=16)
+
+    def collect(i, carry):
+        blocks[first + i] = turned[pl.ds(i, BS, stride=PITCH), :].astype(BF16)
+        return carry
+
+    lax.fori_loop(0, 128, collect, 0, unroll=16)
+
+
+def left(win_ref, blocks, shard):
+    def pair(j, carry):
+        start = pl.multiple_of(HEAD + j * BS, HEAD)
+        both = win_ref[2, shard, pl.ds(start, BS), :].T
+        for half in range(2):
+            i = shard * SHARD + 2 * j + half
+            t = jnp.dot(
+                both[half * BS : (half + 1) * BS, :], blocks[i], preferred_element_type=F32
+            )
+            blocks[i] = t.astype(BF16)
+        return carry
+
+    lax.fori_loop(0, PAIRS, pair, 0, unroll=12)
+
+
+def gather_kernel(
+    p_ref, agg_ref, columns_ref, counts_ref, a_hbm,
+    win_ref, blocks, code_ref, table_ref,
+    raw, own, a_ref, turned, local_sem, send_sem, recv_sem,
+):
     b, g = lax.axis_index("blk"), lax.axis_index("grp")
     core = b % 2
     y, h = g // 2, g % 2
@@ -44,15 +82,20 @@
     barrier = pltpu.get_barrier_semaphore()
     for device in (up_k, down_k, up_y, down_y, across, sibling):
         pl.semaphore_signal(barrier, inc=1, device_id=device, device_id_type=MESH)
+    own[0:HEAD, :] = jnp.zeros((HEAD, 2 * BS), BF16)
+    own[0:HEAD, 0:SHARD] = jnp.broadcast_to(
+        (agg_ref[...] % CB).astype(F32), (HEAD, SHARD)
+    ).astype(BF16)
     load.wait()
-    own[0:HEAD, :] = agg_ref[...]
+    load_a = pltpu.make_async_copy(a_hbm, a_ref, local_sem.at[2])
+    load_a.start()
 
     def pack(j, carry):
         row = pl.multiple_of(HEAD + j * BS, HEAD)
         own[pl.ds(row, BS), :] = jnp.concatenate([raw[2 * j], raw[2 * j + 1]], axis=-1)
         return carry
 
-    lax.fori_loop(0, PAIRS, pack, 0)
+    lax.fori_loop(0, PAIRS, pack, 0, unroll=8)
     keep = pltpu.make_async_copy(own, win_ref.at[2, g], local_sem.at[1])
     keep.start()
     pl.semaphore_wait(barrier, 6)
@@ -107,6 +150,8 @@
     to_y(L_PART, "L", 2, 0, own)
     over((0, LEN), "A", 0, 0, own)
 
+    load_a.wait()
+    turn(a_ref, turned, blocks, 0)
     got(("F", "x"))
     to_y(F_PART, "F", 2, 1)
     to_z(F_PART, "F", 0, 1)
@@ -126,6 +171,7 @@
     for d in (0, 4):
         to_y(L_PART, "L", d, 0)
     over_far(L_PART, "L", 0, 0)
+    turn(a_ref, turned, blocks, 128)
     got(("F", "y+", 2, 1), ("F", "y-", 2, 1))
     on_y(F_HALVES, "F", 2, 1)
     for dy in (-1, 1):
@@ -142,6 +188,8 @@
     on_y(L_HALVES, "L", 2, 1)
     for dy in (-1, 1):
         over((0, LEN), "A", dy, 1)
+    turn(a_ref, turned, blocks, 256)
+    keep.wait()
     got(("L", "f+", 2, 0), ("L", "f-", 2, 0))
     over((0, LEN), "A", 2, 0)
     got(("F", "z+", 0, 0), ("F", "z-", 0, 0))
@@ -153,17 +201,21 @@
         over_far(L_PART, "L", dy, 0)
     got(("L", "f+", 2, 1), ("L", "f-", 2, 1))
     over((0, LEN), "A", 2, 1)
+    for shard in range(0, 2):
+        left(win_ref, blocks, shard)
     got(("F", "z+", 0, 1), ("F", "z-", 0, 1))
     over_far(F_PART, "F", 0, 1)
     for dy in (-1, 1):
         got(("F", "z+", dy, 0), ("F", "z-", dy, 0))
         over_far(F_PART, "F", dy, 0)
+        left(win_ref, blocks, 2 + (dy + 1) // 2)
     for d in (0, 4):
         got(("L", "y+", d, 1), ("L", "y-", d, 1))
         on_y(L_HALVES, "L", d, 1)
     for dy in (-1, 1):
         over_far(L_PART, "L", dy, 1)
-    for dy, dh in ((-1, 1), (1, 1), (2, 0), (2, 1)):
+    for n, (dy, dh) in enumerate(((-1, 1), (1, 1), (2, 0), (2, 1))):
+        left(win_ref, blocks, 4 + n)
         got(("F", "z+", dy, dh), ("F", "z-", dy, dh))
         over_far(F_PART, "F", dy, dh)
     for dh in (0, 1):
@@ -175,89 +227,92 @@
             got(name)
     for copy in copies.values():
         copy.wait_send()
-    keep.wait()
+
+    loc = jnp.mod(columns_ref[...] - (b - 2) * ROWS, PANELS * ROWS)
+    slot = g * SLOTS + lax.broadcasted_iota(jnp.int32, (SLOTS, ROWS), 0)
+    live = slot < counts_ref[...]
+    shard, within = loc // SHARD, loc % SHARD
+    row = shard * LEN + HEAD + within // 2 * BS
+    entry = (shard * 128 + within) * 2 + within % 2
+    code_ref[0:SLOTS, :] = jnp.where(live, row, HEAD)
+    code_ref[SLOTS:, :] = jnp.where(live, entry, SPAN * GROUP * 256)
+    for n in range(SPAN * GROUP):
+        near = win_ref[n // GROUP, n % GROUP, 0:HEAD, :].astype(F32)[0:1].astype(jnp.int32)
+        table_ref[n : n + 1, :] = (near + n // GROUP * CB) * (2 * CB)
+        if n // GROUP == 2:
+            table_ref[n + 32 : n + 33, :] = near * 2
+    table_ref[SPAN * GROUP : 48, :] = jnp.full((8, 128), TARGETS, jnp.int32)
 
 
 COPIES = 86 - 8
 
 
-def gathered(prolong, aggs):
+def gathered(prolong, aggs, columns, counts, a):
+    vmem, hbm = pl.BlockSpec(memory_space=pltpu.VMEM), pl.BlockSpec(memory_space=pltpu.HBM)
     return pl.pallas_call(
         gather_kernel,
-        out_shape=jax.ShapeDtypeStruct((SPAN, GROUP, LEN, 2 * BS), BF16),
-        in_specs=[
-            pl.BlockSpec(memory_space=pl.ANY),
-            pl.BlockSpec(memory_space=pltpu.VMEM),
-        ],
-        out_specs=pl.BlockSpec(memory_space=pl.ANY),
+        out_shape=(
+            pltpu.VMEM((SPAN, GROUP, LEN, 2 * BS), BF16),
+            pltpu.VMEM((ROWS, BS, 2 * BS), BF16),
+            jax.ShapeDtypeStruct((2 * SLOTS, ROWS), jnp.int32),
+            jax.ShapeDtypeStruct((56, 128), jnp.int32),
+        ),
+        in_specs=[hbm, vmem, vmem, vmem, hbm],
+        out_specs=(vmem, vmem, vmem, vmem),
         scratch_shapes=[
             pltpu.VMEM((SHARD, BS, BS), BF16),
             pltpu.VMEM((LEN, 2 * BS), BF16),
-            pltpu.SemaphoreType.DMA((2,)),
+            pltpu.VMEM((SLOTS, BS, BS, ROWS), BF16),
+            pltpu.VMEM((BS * PITCH, 128), F32),
+            pltpu.SemaphoreType.DMA((3,)),
             pltpu.SemaphoreType.DMA((COPIES,)),
             pltpu.SemaphoreType.DMA((COPIES,)),
         ],
-        compiler_params=pltpu.CompilerParams(collective_id=0, has_side_effects=True),
+        compiler_params=pltpu.CompilerParams(
+            collective_id=0, has_side_effects=True, vmem_limit_bytes=20 * 2**20
+        ),
         name="gather_window",
-    )(prolong, aggs)
-
-
-def compute_kernel(
-    row_ref, loc_ref, base_ref, tj_ref, a_ref, win_ref, part_ref, turned, blocks, acc
-):
+    )(
+        pltpu.with_memory_space_constraint(prolong, pltpu.HBM),
+        aggs,
+        columns,
+        counts,
+        pltpu.with_memory_space_constraint(a, pltpu.HBM),
+    )
+
+
+def compute_kernel(code_ref, table_ref, win_ref, blocks, part_ref, acc):
     def clear(t, carry):
         acc[t] = jnp.zeros((BS, 2 * BS), F32)
         return carry
 
-    lax.fori_loop(0, ACCS, clear, 0)
-
-    for first in range(0, ROWS, 128):
-
-        def turn(r, carry, first=first):
-            both = jnp.concatenate(
-                [a_ref[s, r, :, first : first + 128] for s in range(SLOTS)], axis=0
+    lax.fori_loop(0, ACCS, clear, 0, unroll=8)
+
+    for shard in range(GROUP):
+
+        def right(j, carry, shard=shard):
+            i = shard * SHARD + j
+            none = jnp.zeros((BS, 2 * BS), BF16)
+            column = table_ref[(48 + shard) * 128 + j]
+            targets, picked = [], []
+            for s in range(SLOTS):
+                row = pl.multiple_of(code_ref[s, i], HEAD)
+                entry = code_ref[SLOTS + s, i]
+                picked.append(win_ref[pl.ds(row, BS), :])
+                targets.append(table_ref[entry // 2] + column + entry % 2)
+            stack = jnp.concatenate(
+                [
+                    jnp.concatenate([picked[0], none], axis=1),
+                    jnp.concatenate([none, picked[1]], axis=1),
+                ],
+                axis=0,
             )
-            turned[pl.ds(pl.multiple_of(r * 128, 128), 128), :] = both.astype(F32).T
+            r = jnp.dot(blocks[i], stack, preferred_element_type=F32)
+            acc[targets[0]] += r[:, : 2 * BS]
+            acc[targets[1]] += r[:, 2 * BS :]
             return carry
 
-        lax.fori_loop(0, BS, turn, 0, unroll=4)
-
-        def collect(i, carry, first=first):
-            blocks[first + i] = turned[pl.ds(i, BS, stride=128), :].astype(BF16)
-            return carry
-
-        lax.fori_loop(0, 128, collect, 0, unroll=8)
-
-    for shard in range(GROUP):
-
-        def left(j, carry, shard=shard):
-            start = (2 * GROUP + shard) * LEN + HEAD + j * BS
-            both = win_ref[pl.ds(pl.multiple_of(start, HEAD), BS), :].T
-            for half in range(2):
-                i = shard * SHARD + 2 * j + half
-                t = jnp.dot(
-                    both[half * BS : (half + 1) * BS, :],
-                    blocks[i],
-                    preferred_element_type=F32,
-                )
-                blocks[i] = t.astype(BF16)
-            return carry
-
-        lax.fori_loop(0, PAIRS, left, 0, unroll=4)
-
-    def right(i, carry):
-        t = blocks[i]
-        none = jnp.zeros((BS, 2 * BS), BF16)
-        for s in range(SLOTS):
-            row = pl.multiple_of(row_ref[s, i], HEAD)
-            picked = win_ref[pl.ds(row, BS), :]
-            stack = [picked, none] if s == 0 else [none, picked]
-            r = jnp.dot(t, jnp.concatenate(stack, axis=0), preferred_element_type=F32)
-            target = tj_ref[loc_ref[s, i]] + base_ref[s, i]
-            acc[target] += r
-        return carry
-
-    lax.fori_loop(0, ROWS, right, 0, unroll=4)
+        lax.fori_loop(0, SHARD, right, 0, unroll=16)
 
     low = lax.broadcasted_iota(jnp.int32, (BS, 2 * BS), 1) < BS
 
@@ -269,25 +324,21 @@
         part_ref[t] = jnp.where(low, first, second)
         return carry
 
-    lax.fori_loop(0, BLOCKS, fold, 0)
-
-
-def computed(rows, locs, bases, tj, a, win):
+    lax.fori_loop(0, BLOCKS, fold, 0, unroll=4)
+
+
+def computed(codes, table, win, blocks):
     smem = pl.BlockSpec(memory_space=pltpu.SMEM)
     vmem = pl.BlockSpec(memory_space=pltpu.VMEM)
     return pl.pallas_call(
         compute_kernel,
-        out_shape=jax.ShapeDtypeStruct((BLOCKS, BS, 2 * BS), F32),
-        in_specs=[smem, smem, smem, smem, vmem, vmem],
+        out_shape=pltpu.VMEM((BLOCKS, BS, 2 * BS), F32),
+        in_specs=[smem, smem, vmem, vmem],
         out_specs=vmem,
-        scratch_shapes=[
-            pltpu.VMEM((BS * 128, 128), F32),
-            pltpu.VMEM((ROWS, BS, 2 * BS), BF16),
-            pltpu.VMEM((ACCS, BS, 2 * BS), F32),
-        ],
-        compiler_params=pltpu.CompilerParams(vmem_limit_bytes=56 * 2**20),
-        name="triple_products",
-    )(rows, locs, bases, tj, a, win)
+        scratch_shapes=[pltpu.VMEM((ACCS, BS, 2 * BS), F32)],
+        compiler_params=pltpu.CompilerParams(vmem_limit_bytes=16 * 2**20),
+        name="right_products",
+    )(codes, table, win, blocks)
 
 
 def reduce_kernel(part_ref, out_ref, landed, total, placed, send_sem, recv_sem, send2, recv2):
@@ -386,31 +437,23 @@
             pltpu.SemaphoreType.DMA((SHARE,)),
             pltpu.SemaphoreType.DMA((BLOCKS,)),
         ],
-        compiler_params=pltpu.CompilerParams(collective_id=1, has_side_effects=True),
+        compiler_params=pltpu.CompilerParams(
+            collective_id=1, has_side_effects=True, vmem_limit_bytes=12 * 2**20
+        ),
         name="reduce_blocks",
     )(part)
 
 
 def local(block_values, block_columns, row_counts, prolong_blocks, aggregates):
-    b, g = lax.axis_index("blk"), lax.axis_index("grp")
-    head = jnp.pad((aggregates % CB).astype(BF16)[None, :], ((0, HEAD - 1), (0, 2 * BS - SHARD)))
-    win = gathered(prolong_blocks, head)
-
-    loc = jnp.mod(block_columns.T - (b - 2) * ROWS, PANELS * ROWS)
-    slot = g * SLOTS + jnp.arange(SLOTS, dtype=jnp.int32)
-    live = slot[:, None] < row_counts[None, :]
-    loc = jnp.where(live, loc, SPAN * ROWS)
-    rows = (loc // SHARD) * LEN + HEAD + (loc % SHARD) // 2 * BS
-    rows = jnp.where(live, rows, HEAD)
-
-    near = win[:, :, 0, :SHARD].astype(jnp.int32).reshape(SPAN, ROWS)
-    tj = (jnp.arange(SPAN, dtype=jnp.int32)[:, None] * CB + near) * (2 * CB)
-    tj = jnp.concatenate([tj.reshape(-1), jnp.full((128,), TARGETS, jnp.int32)])
-    bases = jnp.where(live, near[2][None, :] * 2 + loc % 2, 0)
-
-    a = jnp.transpose(block_values, (1, 2, 3, 0))
-    part = computed(rows, loc, bases, tj, a, win.reshape(-1, 2 * BS))
-    return reduced(part)
+    win, blocks, codes, table = gathered(
+        prolong_blocks,
+        aggregates[None, :],
+        block_columns.T,
+        row_counts[None, :],
+        jnp.transpose(block_values, (1, 2, 3, 0)),
+    )
+    win = win.reshape(-1, 2 * BS)
+    return reduced(computed(codes, table.reshape(-1), win, blocks))
 
 
 def solution(mesh):

time: 168 us -> 116 us (0.69)
  Pallas kernels: 158 us -> 111 us
  other arithmetic: 3.73 us -> 0 us
    pallas_call x2, Pallas kernels: 124 us -> 80.9 us  [the longest x1 67.1 us: gathered(): pl.pallas_call(gather_kernel, out_shape=(pltpu.VMEM((SPAN, GROUP, LEN, 2...]
    pallas_call x1, Pallas kernels: 33.9 us -> 30.1 us  [reduced(): pl.pallas_call(reduce_kernel, out_shape=jax.ShapeDtypeStruct((GROUP, CB,...]
where the time goes in v2:
time: 116 us; the launch traced here: 114 us
  Pallas kernels  111 us (96%)
  local copies, waits for them, and re-layouts  2.99 us (3%)
    pallas_call x1, Pallas kernels, gathered(): pl.pallas_call(gather_kernel, out_shape=(pltpu.VMEM((SPAN, GROUP, LEN, 2...  67.1 us
    pallas_call x1, Pallas kernels, reduced(): pl.pallas_call(reduce_kernel, out_shape=jax.ShapeDtypeStruct((GROUP, CB,...  30.1 us
    pallas_call x1, Pallas kernels, computed(): pl.pallas_call(compute_kernel, out_shape=pltpu.VMEM((BLOCKS, BS, 2 * BS),...  13.8 us

profile of v2, /device:TPU:0, one launch (start us, length us, event | category | flops | bytes accessed | tf_op | source)
XLA Modules:
  0.0 114.1 jit_solution(13214674984205472088)
XLA Ops:
  0.0 0.7 broadcast_in_dim.7.counts_ref
  0.7 0.0 copy-start
  0.7 0.7 copy-done
  1.4 0.0 copy-start.1
  1.4 0.7 copy-done.1
  2.0 67.1 %gather_window.1 = (bf16[5,8,1552,128]{3,2,1,0:T(8,128)(2,1)S(1)}, bf16[384,64,128]{2,1,0:T(8,128)(2,1)S(1)}, s32[4,384]{1,0:T(4,128)S(1)}, s32[56,128]{1,0:T(8,128)S(1)}) custom-call(bf16[48,64,64]{2,1,0:T(8,128)(2,1)} %p_ref.1, s32[1,48]{1,0:T(1,128)S(1)} %bitcast.8, s32[2,384]{1,0:T(2,128)S(1)} %bitcast.7, s32[1,384]{1,0:T(1,128)S(1)} %broadcast_in_dim.7.counts_ref, ...), custom_call_target="tpu_custom_call" | custom-call | tf_op jit(solution)/shard_map/gather_window/pallas_call | solution.py:252
  69.1 13.8 %right_products.1.part_ref = f32[40,64,128]{2,1,0:T(8,128)S(1)} custom-call(s32[4,384]{1,0:T(4,128)S(1)} %get-tuple-element.9.code_ref, s32[7168]{0:T(1024)S(1)} %bitcast.6, bf16[62080,128]{1,0:T(8,128)(2,1)S(1)} %bitcast.5, bf16[384,64,128]{2,1,0:T(8,128)(2,1)S(1)} %get-tuple-element.12.blocks), custom_call_target="tpu_custom_call" | custom-call | tf_op jit(solution)/shard_map/right_products/pallas_call | solution.py:333
  83.0 30.1 %reduce_blocks.1 = f32[8,4,64,64]{3,2,1,0:T(8,128)S(1)} custom-call(f32[40,64,128]{2,1,0:T(8,128)S(1)} %right_products.1.part_ref), custom_call_target="tpu_custom_call" | custom-call | tf_op jit(solution)/shard_map/reduce_blocks/pallas_call | solution.py:426
  113.1 1.0 copy.7
Async XLA Ops:
  0.7 0.7 copy-start
  1.4 0.7 copy-start.1

commit v3 on v2

--- a/solution.py
+++ b/solution.py
@@ -28,7 +28,6 @@
 TARGETS = SPAN * CB * CB * 2
 ACCS = TARGETS + 8
 BLOCKS = TARGETS // 4
-SHARE = BLOCKS // GROUP
 PITCH = 136
 
 
@@ -66,25 +65,45 @@
 
 
 def gather_kernel(
-    p_ref, agg_ref, columns_ref, counts_ref, a_hbm,
+    p_ref, agg_hbm, columns_hbm, counts_hbm, a_hbm,
     win_ref, blocks, code_ref, table_ref,
-    raw, own, a_ref, turned, local_sem, send_sem, recv_sem,
+    raw, own, a_ref, turned, agg_ref, columns_ref, counts_ref,
+    local_sem, send_sem, recv_sem,
 ):
     b, g = lax.axis_index("blk"), lax.axis_index("grp")
     core = b % 2
     y, h = g // 2, g % 2
-    up_k, down_k = ((b + 2) % PANELS, g), ((b + PANELS - 2) % PANELS, g)
+    other = g + 1 - 2 * h
+    z = (b // 2) % 4
+    up_end = jnp.where(z == 3, 1, 0)
+    down_end = jnp.where(z == 0, 1, 0)
+
+    def on_k(step, end, dh):
+        return (b + step + PANELS) % PANELS, g + dh * end * (1 - 2 * h)
+
     up_y, down_y = (b, (g + 2) % GROUP), (b, (g + GROUP - 2) % GROUP)
-    across, sibling = (b, g + 1 - 2 * h), (b + 1 - 2 * core, g)
+    across, sibling = (b, other), (b + 1 - 2 * core, g)
 
     load = pltpu.make_async_copy(p_ref, raw, local_sem.at[0])
     load.start()
+    small = [
+        pltpu.make_async_copy(source, target, local_sem.at[3 + n])
+        for n, (source, target) in enumerate(
+            ((agg_hbm, agg_ref), (columns_hbm, columns_ref), (counts_hbm, counts_ref))
+        )
+    ]
+    for copy in small:
+        copy.start()
     barrier = pltpu.get_barrier_semaphore()
-    for device in (up_k, down_k, up_y, down_y, across, sibling):
+    greeted = [up_y, down_y, across, sibling]
+    for step in (2, PANELS - 2):
+        greeted += [((b + step) % PANELS, column) for column in (g, other)]
+    for device in greeted:
         pl.semaphore_signal(barrier, inc=1, device_id=device, device_id_type=MESH)
+    small[0].wait()
     own[0:HEAD, :] = jnp.zeros((HEAD, 2 * BS), BF16)
     own[0:HEAD, 0:SHARD] = jnp.broadcast_to(
-        (agg_ref[...] % CB).astype(F32), (HEAD, SHARD)
+        (agg_ref[...] % CB).astype(F32).reshape(1, SHARD), (HEAD, SHARD)
     ).astype(BF16)
     load.wait()
     load_a = pltpu.make_async_copy(a_hbm, a_ref, local_sem.at[2])
@@ -98,7 +117,7 @@
     lax.fori_loop(0, PAIRS, pack, 0, unroll=8)
     keep = pltpu.make_async_copy(own, win_ref.at[2, g], local_sem.at[1])
     keep.start()
-    pl.semaphore_wait(barrier, 6)
+    pl.semaphore_wait(barrier, len(greeted))
 
     copies = {}
 
@@ -133,8 +152,9 @@
         send((tag, "f-", d, dh), halves[1], d, 1, dh, d, down_y)
 
     def to_z(part, tag, dy, dh, src=None):
-        send((tag, "z+", dy, dh), part, 2, dy, dh, 0, up_k, src)
-        send((tag, "z-", dy, dh), part, 2, dy, dh, 4, down_k, src)
+        for sign, step, end, to_d in (("z+", 2, up_end, 0), ("z-", -2, down_end, 4)):
+            column = dh * (1 - end)
+            send((tag, sign, dy, dh), part, 2, dy, column, to_d, on_k(step, end, dh), src)
 
     def over(part, tag, dy, dh, src=None):
         send((tag, "s", dy, dh), part, 2, dy, dh, 1 + 2 * core, sibling, src)
@@ -154,6 +174,7 @@
     turn(a_ref, turned, blocks, 0)
     got(("F", "x"))
     to_y(F_PART, "F", 2, 1)
+    keep.wait()
     to_z(F_PART, "F", 0, 1)
     got(("F", "y+", 2, 0), ("F", "y-", 2, 0))
     on_y(F_HALVES, "F", 2, 0)
@@ -189,7 +210,6 @@
     for dy in (-1, 1):
         over((0, LEN), "A", dy, 1)
     turn(a_ref, turned, blocks, 256)
-    keep.wait()
     got(("L", "f+", 2, 0), ("L", "f-", 2, 0))
     over((0, LEN), "A", 2, 0)
     got(("F", "z+", 0, 0), ("F", "z-", 0, 0))
@@ -228,9 +248,11 @@
     for copy in copies.values():
         copy.wait_send()
 
+    for copy in small[1:]:
+        copy.wait()
     loc = jnp.mod(columns_ref[...] - (b - 2) * ROWS, PANELS * ROWS)
     slot = g * SLOTS + lax.broadcasted_iota(jnp.int32, (SLOTS, ROWS), 0)
-    live = slot < counts_ref[...]
+    live = slot < counts_ref[...].reshape(1, ROWS)
     shard, within = loc // SHARD, loc % SHARD
     row = shard * LEN + HEAD + within // 2 * BS
     entry = (shard * 128 + within) * 2 + within % 2
@@ -257,14 +279,17 @@
             jax.ShapeDtypeStruct((2 * SLOTS, ROWS), jnp.int32),
             jax.ShapeDtypeStruct((56, 128), jnp.int32),
         ),
-        in_specs=[hbm, vmem, vmem, vmem, hbm],
+        in_specs=[hbm] * 5,
         out_specs=(vmem, vmem, vmem, vmem),
         scratch_shapes=[
             pltpu.VMEM((SHARD, BS, BS), BF16),
             pltpu.VMEM((LEN, 2 * BS), BF16),
             pltpu.VMEM((SLOTS, BS, BS, ROWS), BF16),
             pltpu.VMEM((BS * PITCH, 128), F32),
-            pltpu.SemaphoreType.DMA((3,)),
+            pltpu.VMEM((SHARD,), jnp.int32),
+            pltpu.VMEM((SLOTS, ROWS), jnp.int32),
+            pltpu.VMEM((ROWS,), jnp.int32),
+            pltpu.SemaphoreType.DMA((6,)),
             pltpu.SemaphoreType.DMA((COPIES,)),
             pltpu.SemaphoreType.DMA((COPIES,)),
         ],
@@ -272,13 +297,7 @@
             collective_id=0, has_side_effects=True, vmem_limit_bytes=20 * 2**20
         ),
         name="gather_window",
-    )(
-        pltpu.with_memory_space_constraint(prolong, pltpu.HBM),
-        aggs,
-        columns,
-        counts,
-        pltpu.with_memory_space_constraint(a, pltpu.HBM),
-    )
+    )(*(pltpu.with_memory_space_constraint(x, pltpu.HBM) for x in (prolong, aggs, columns, counts, a)))
 
 
 def compute_kernel(code_ref, table_ref, win_ref, blocks, part_ref, acc):
@@ -321,7 +340,7 @@
         three, four = acc[4 * t + 2], acc[4 * t + 3]
         first = one + pltpu.roll(two, BS, 1)
         second = pltpu.roll(three, BS, 1) + four
-        part_ref[t] = jnp.where(low, first, second)
+        part_ref[t % GROUP * SPAN + t // GROUP] = jnp.where(low, first, second)
         return carry
 
     lax.fori_loop(0, BLOCKS, fold, 0, unroll=4)
@@ -351,7 +370,7 @@
     first = []
     for n, other in enumerate(others):
         copy = pltpu.make_async_remote_copy(
-            src_ref=part_ref.at[pl.ds(other * SHARE, SHARE)],
+            src_ref=part_ref.at[pl.ds(other * SPAN, SPAN)],
             dst_ref=landed.at[n],
             send_sem=send_sem.at[n],
             recv_sem=recv_sem.at[n],
@@ -361,61 +380,61 @@
         copy.start()
         first.append(copy)
     out_ref[...] = jnp.zeros(out_ref.shape, F32)
-    total[...] = part_ref[pl.ds(g * SHARE, SHARE)]
+    total[...] = part_ref[pl.ds(g * SPAN, SPAN)]
     for n, copy in enumerate(first):
         copy.wait_recv()
         total[...] += landed[n]
 
-    def owner(m):
-        panel = (b + PANELS - 2 + m // 8) % PANELS
-        return panel, panel // 2
-
-    def hop(e, m, device):
-        return pltpu.make_async_remote_copy(
-            src_ref=total.at[e],
-            dst_ref=placed.at[m],
-            send_sem=send2.at[e],
-            recv_sem=recv2.at[m],
-            device_id=(b, device),
+    def hop(d):
+        panel = (b + PANELS - 2 + d) % PANELS
+        owner, side = panel // 2, panel % 2
+        copy = pltpu.make_async_remote_copy(
+            src_ref=total.at[d],
+            dst_ref=placed.at[side, g],
+            send_sem=send2.at[d],
+            recv_sem=recv2.at[side],
+            device_id=(b, owner),
             device_id_type=MESH,
         )
-
-    def keep(panel, m, block):
-        row = (panel % 2) * CB + (m % 8) // 2
-        column = (m % 2) * 2
-        out_ref[row, column] = block[:, :BS]
-        out_ref[row, column + 1] = block[:, BS:]
-
-    for e in range(SHARE):
-        m = g * SHARE + e
-        panel, device = owner(m)
-
-        @pl.when(device != g)
-        def _(e=e, m=m, device=device):
-            hop(e, m, device).start()
-
-        @pl.when(device == g)
-        def _(e=e, m=m, panel=panel):
-            keep(panel, m, total[e])
-
-    def arrive(m, carry):
-        panel, device = owner(m)
-
-        @pl.when(jnp.logical_and(device == g, m // SHARE != g))
-        def _():
-            hop(0, m, (g + 1) % GROUP).wait_recv()
-            keep(panel, m, placed[m])
-
-        return carry
-
-    lax.fori_loop(0, BLOCKS, arrive, 0)
-    for e in range(SHARE):
-        m = g * SHARE + e
-        panel, device = owner(m)
-
-        @pl.when(device != g)
-        def _(e=e, m=m, device=device):
-            hop(e, m, device).wait_send()
+        return owner, side, copy
+
+    for d in range(SPAN):
+        owner, side, copy = hop(d)
+
+        @pl.when(owner != g)
+        def _(copy=copy):
+            copy.start()
+
+        @pl.when(owner == g)
+        def _(d=d, side=side):
+            placed[side, g] = total[d]
+
+    for side in range(2):
+        d = (2 * g + side + PANELS + 2 - b) % PANELS
+
+        @pl.when(d < SPAN)
+        def _(side=side):
+            rest = placed.at[side, pl.ds(0, GROUP - 1)]
+            pltpu.make_async_remote_copy(
+                src_ref=rest,
+                dst_ref=rest,
+                send_sem=send2.at[0],
+                recv_sem=recv2.at[side],
+                device_id=(b, others[0]),
+                device_id_type=MESH,
+            ).wait_recv()
+            for n in range(GROUP):
+                block = placed[side, n]
+                row, column = side * CB + n // 2, n % 2 * 2
+                out_ref[row, column] = block[:, :BS]
+                out_ref[row, column + 1] = block[:, BS:]
+
+    for d in range(SPAN):
+        owner, side, copy = hop(d)
+
+        @pl.when(owner != g)
+        def _(copy=copy):
+            copy.wait_send()
 
     for copy in first:
         copy.wait_send()
@@ -429,13 +448,13 @@
         in_specs=[vmem],
         out_specs=vmem,
         scratch_shapes=[
-            pltpu.VMEM((GROUP - 1, SHARE, BS, 2 * BS), F32),
-            pltpu.VMEM((SHARE, BS, 2 * BS), F32),
-            pltpu.VMEM((BLOCKS, BS, 2 * BS), F32),
+            pltpu.VMEM((GROUP - 1, SPAN, BS, 2 * BS), F32),
+            pltpu.VMEM((SPAN, BS, 2 * BS), F32),
+            pltpu.VMEM((2, GROUP, BS, 2 * BS), F32),
             pltpu.SemaphoreType.DMA((GROUP - 1,)),
             pltpu.SemaphoreType.DMA((GROUP - 1,)),
-            pltpu.SemaphoreType.DMA((SHARE,)),
-            pltpu.SemaphoreType.DMA((BLOCKS,)),
+            pltpu.SemaphoreType.DMA((SPAN,)),
+            pltpu.SemaphoreType.DMA((2,)),
         ],
         compiler_params=pltpu.CompilerParams(
             collective_id=1, has_side_effects=True, vmem_limit_bytes=12 * 2**20
@@ -447,9 +466,9 @@
 def local(block_values, block_columns, row_counts, prolong_blocks, aggregates):
     win, blocks, codes, table = gathered(
         prolong_blocks,
-        aggregates[None, :],
+        aggregates,
         block_columns.T,
-        row_counts[None, :],
+        row_counts,
         jnp.transpose(block_values, (1, 2, 3, 0)),
     )
     win = win.reshape(-1, 2 * BS)

time: 116 us -> 109 us (0.940); the launches traced: 114 us -> 108 us
  Pallas kernels: 111 us -> 107 us
  local copies, waits for them, and re-layouts: 2.99 us -> 0.97 us
    pallas_call x1, Pallas kernels: 67.1 us -> 64.8 us  [gathered(): pl.pallas_call(gather_kernel, out_shape=(pltpu.VMEM((SPAN, GROUP, LEN, 2...]
    unnamed x5 -> x1, local copies, waits for them, and re-layouts: 2.31 us -> 0.97 us
    pallas_call x1, Pallas kernels: 30.1 us -> 28.8 us  [reduced(): pl.pallas_call(reduce_kernel, out_shape=jax.ShapeDtypeStruct((GROUP, CB,...]
where the time goes in v3:
time: 109 us; the launch traced here: 108 us
  Pallas kernels  107 us (98%)
    pallas_call x1, Pallas kernels, gathered(): pl.pallas_call(gather_kernel, out_shape=(pltpu.VMEM((SPAN, GROUP, LEN, 2...  64.8 us
    pallas_call x1, Pallas kernels, reduced(): pl.pallas_call(reduce_kernel, out_shape=jax.ShapeDtypeStruct((GROUP, CB,...  28.8 us
    pallas_call x1, Pallas kernels, computed(): pl.pallas_call(compute_kernel, out_shape=pltpu.VMEM((BLOCKS, BS, 2 * BS),...  13.8 us

profile of v3, /device:TPU:0, one launch (start us, length us, event | category | flops | bytes accessed | tf_op | source)
XLA Modules:
  0.0 108.5 jit_solution(1525193151060028653)
XLA Ops:
  0.0 64.8 %gather_window.1 = (bf16[5,8,1552,128]{3,2,1,0:T(8,128)(2,1)S(1)}, bf16[384,64,128]{2,1,0:T(8,128)(2,1)S(1)}, s32[4,384]{1,0:T(4,128)S(1)}, s32[56,128]{1,0:T(8,128)S(1)}) custom-call(bf16[48,64,64]{2,1,0:T(8,128)(2,1)} %p_ref.1, s32[48]{0:T(128)} %agg_hbm.1, s32[2,384]{1,0:T(2,128)} %bitcast.7, s32[384]{0:T(512)} %counts_hbm.1, bf16[2,64,64,384]{3,2,1,0:T(8,128)(2,1)} %bitcast.6), custom_call_target="tpu_custom_call" | custom-call | tf_op jit(solution)/shard_map/gather_window/pallas_call | solution.py:274
  64.8 13.8 %right_products.1.part_ref = f32[40,64,128]{2,1,0:T(8,128)S(1)} custom-call(s32[4,384]{1,0:T(4,128)S(1)} %get-tuple-element.9.code_ref, s32[7168]{0:T(1024)S(1)} %bitcast.5, bf16[62080,128]{1,0:T(8,128)(2,1)S(1)} %bitcast.4, bf16[384,64,128]{2,1,0:T(8,128)(2,1)S(1)} %get-tuple-element.12.blocks), custom_call_target="tpu_custom_call" | custom-call | tf_op jit(solution)/shard_map/right_products/pallas_call | solution.py:352
  78.6 28.8 %reduce_blocks.1 = f32[8,4,64,64]{3,2,1,0:T(8,128)S(1)} custom-call(f32[40,64,128]{2,1,0:T(8,128)S(1)} %right_products.1.part_ref), custom_call_target="tpu_custom_call" | custom-call | tf_op jit(solution)/shard_map/reduce_blocks/pallas_call | solution.py:445
  107.5 1.0 copy.7

commit v4 on v3

--- a/solution.py
+++ b/solution.py
@@ -20,10 +20,10 @@
 SPAN = 5
 HEAD = 16
 LEN = HEAD + PAIRS * BS
-CUT = HEAD + 14 * BS
+CUT = HEAD + 13 * BS
 F_PART, L_PART = (0, CUT), (CUT, LEN - CUT)
-F_HALVES = ((0, 448), (448, CUT - 448))
-L_HALVES = ((CUT, 320), (CUT + 320, 320))
+F_HALVES = ((0, 416), (416, CUT - 416))
+L_HALVES = ((CUT, 352), (CUT + 352, 352))
 SLOTS = 2
 TARGETS = SPAN * CB * CB * 2
 ACCS = TARGETS + 8
@@ -300,7 +300,7 @@
     )(*(pltpu.with_memory_space_constraint(x, pltpu.HBM) for x in (prolong, aggs, columns, counts, a)))
 
 
-def compute_kernel(code_ref, table_ref, win_ref, blocks, part_ref, acc):
+def compute_kernel(code_ref, table_ref, win_ref, blocks, part_ref, short_ref, acc):
     def clear(t, carry):
         acc[t] = jnp.zeros((BS, 2 * BS), F32)
         return carry
@@ -331,7 +331,7 @@
             acc[targets[1]] += r[:, 2 * BS :]
             return carry
 
-        lax.fori_loop(0, SHARD, right, 0, unroll=16)
+        lax.fori_loop(0, SHARD, right, 0, unroll=SHARD)
 
     low = lax.broadcasted_iota(jnp.int32, (BS, 2 * BS), 1) < BS
 
@@ -340,7 +340,10 @@
         three, four = acc[4 * t + 2], acc[4 * t + 3]
         first = one + pltpu.roll(two, BS, 1)
         second = pltpu.roll(three, BS, 1) + four
-        part_ref[t % GROUP * SPAN + t // GROUP] = jnp.where(low, first, second)
+        place = t % GROUP * SPAN + t // GROUP
+        block = jnp.where(low, first, second)
+        part_ref[place] = block
+        short_ref[place] = block.astype(BF16)
         return carry
 
     lax.fori_loop(0, BLOCKS, fold, 0, unroll=4)
@@ -351,16 +354,22 @@
     vmem = pl.BlockSpec(memory_space=pltpu.VMEM)
     return pl.pallas_call(
         compute_kernel,
-        out_shape=pltpu.VMEM((BLOCKS, BS, 2 * BS), F32),
+        out_shape=(
+            pltpu.VMEM((BLOCKS, BS, 2 * BS), F32),
+            pltpu.VMEM((BLOCKS, BS, 2 * BS), BF16),
+        ),
         in_specs=[smem, smem, vmem, vmem],
-        out_specs=vmem,
+        out_specs=(vmem, vmem),
         scratch_shapes=[pltpu.VMEM((ACCS, BS, 2 * BS), F32)],
         compiler_params=pltpu.CompilerParams(vmem_limit_bytes=16 * 2**20),
         name="right_products",
     )(codes, table, win, blocks)
 
 
-def reduce_kernel(part_ref, out_ref, landed, total, placed, send_sem, recv_sem, send2, recv2):
+def reduce_kernel(
+    part_ref, short_ref, out_ref, landed, landed_short, total, placed,
+    send_sem, recv_sem, send2, recv2,
+):
     b, g = lax.axis_index("blk"), lax.axis_index("grp")
     others = [(g + n) % GROUP for n in range(1, GROUP)]
     barrier = pltpu.get_barrier_semaphore()
@@ -369,9 +378,10 @@
     pl.semaphore_wait(barrier, GROUP - 1)
     first = []
     for n, other in enumerate(others):
+        source, target = (part_ref, landed) if n % 2 else (short_ref, landed_short)
         copy = pltpu.make_async_remote_copy(
-            src_ref=part_ref.at[pl.ds(other * SPAN, SPAN)],
-            dst_ref=landed.at[n],
+            src_ref=source.at[pl.ds(other * SPAN, SPAN)],
+            dst_ref=target.at[n // 2],
             send_sem=send_sem.at[n],
             recv_sem=recv_sem.at[n],
             device_id=(b, other),
@@ -383,7 +393,7 @@
     total[...] = part_ref[pl.ds(g * SPAN, SPAN)]
     for n, copy in enumerate(first):
         copy.wait_recv()
-        total[...] += landed[n]
+        total[...] += (landed if n % 2 else landed_short)[n // 2].astype(F32)
 
     def hop(d):
         panel = (b + PANELS - 2 + d) % PANELS
@@ -440,15 +450,16 @@
         copy.wait_send()
 
 
-def reduced(part):
+def reduced(part, short):
     vmem = pl.BlockSpec(memory_space=pltpu.VMEM)
     return pl.pallas_call(
         reduce_kernel,
         out_shape=jax.ShapeDtypeStruct((GROUP, CB, BS, BS), F32),
-        in_specs=[vmem],
+        in_specs=[vmem, vmem],
         out_specs=vmem,
         scratch_shapes=[
-            pltpu.VMEM((GROUP - 1, SPAN, BS, 2 * BS), F32),
+            pltpu.VMEM((GROUP // 2 - 1, SPAN, BS, 2 * BS), F32),
+            pltpu.VMEM((GROUP // 2, SPAN, BS, 2 * BS), BF16),
             pltpu.VMEM((SPAN, BS, 2 * BS), F32),
             pltpu.VMEM((2, GROUP, BS, 2 * BS), F32),
             pltpu.SemaphoreType.DMA((GROUP - 1,)),
@@ -460,7 +471,7 @@
             collective_id=1, has_side_effects=True, vmem_limit_bytes=12 * 2**20
         ),
         name="reduce_blocks",
-    )(part)
+    )(part, short)
 
 
 def local(block_values, block_columns, row_counts, prolong_blocks, aggregates):
@@ -472,7 +483,7 @@
         jnp.transpose(block_values, (1, 2, 3, 0)),
     )
     win = win.reshape(-1, 2 * BS)
-    return reduced(computed(codes, table.reshape(-1), win, blocks))
+    return reduced(*computed(codes, table.reshape(-1), win, blocks))
 
 
 def solution(mesh):

time: 109 us -> 101 us (0.927)
  Pallas kernels: 107 us -> 98.7 us
    pallas_call x1, Pallas kernels: 13.8 us -> 9.18 us  [computed(): pl.pallas_call(compute_kernel, out_shape=(pltpu.VMEM((BLOCKS, BS, 2 * BS)...]
    pallas_call x1, Pallas kernels: 28.8 us -> 25.7 us  [reduced(): pl.pallas_call(reduce_kernel, out_shape=jax.ShapeDtypeStruct((GROUP, CB,...]
where the time goes in v4:
time: 101 us; the launch traced here: 99.7 us
  Pallas kernels  98.7 us (98%)
    pallas_call x1, Pallas kernels, gathered(): pl.pallas_call(gather_kernel, out_shape=(pltpu.VMEM((SPAN, GROUP, LEN, 2...  63.8 us
    pallas_call x1, Pallas kernels, reduced(): pl.pallas_call(reduce_kernel, out_shape=jax.ShapeDtypeStruct((GROUP, CB,...  25.7 us
    pallas_call x1, Pallas kernels, computed(): pl.pallas_call(compute_kernel, out_shape=(pltpu.VMEM((BLOCKS, BS, 2 * BS)...  9.18 us

profile of v4, /device:TPU:0, one launch (start us, length us, event | category | flops | bytes accessed | tf_op | source)
XLA Modules:
  0.0 99.7 jit_solution(17761768193018250186)
XLA Ops:
  0.0 63.8 %gather_window.1 = (bf16[5,8,1552,128]{3,2,1,0:T(8,128)(2,1)S(1)}, bf16[384,64,128]{2,1,0:T(8,128)(2,1)S(1)}, s32[4,384]{1,0:T(4,128)S(1)}, s32[56,128]{1,0:T(8,128)S(1)}) custom-call(bf16[48,64,64]{2,1,0:T(8,128)(2,1)} %p_ref.1, s32[48]{0:T(128)} %agg_hbm.1, s32[2,384]{1,0:T(2,128)} %bitcast.7, s32[384]{0:T(512)} %counts_hbm.1, bf16[2,64,64,384]{3,2,1,0:T(8,128)(2,1)} %bitcast.6), custom_call_target="tpu_custom_call" | custom-call | tf_op jit(solution)/shard_map/gather_window/pallas_call | solution.py:274
  63.8 9.2 %right_products.1 = (f32[40,64,128]{2,1,0:T(8,128)S(1)}, bf16[40,64,128]{2,1,0:T(8,128)(2,1)S(1)}) custom-call(s32[4,384]{1,0:T(4,128)S(1)} %get-tuple-element.11.code_ref, s32[7168]{0:T(1024)S(1)} %bitcast.5, bf16[62080,128]{1,0:T(8,128)(2,1)S(1)} %bitcast.4, bf16[384,64,128]{2,1,0:T(8,128)(2,1)S(1)} %get-tuple-element.14.blocks), custom_call_target="tpu_custom_call" | custom-call | tf_op jit(solution)/shard_map/right_products/pallas_call | solution.py:355
  73.0 25.7 %reduce_blocks.1 = f32[8,4,64,64]{3,2,1,0:T(8,128)S(1)} custom-call(f32[40,64,128]{2,1,0:T(8,128)S(1)} %get-tuple-element.15.part_ref, bf16[40,64,128]{2,1,0:T(8,128)(2,1)S(1)} %get-tuple-element.16.short_ref), custom_call_target="tpu_custom_call" | custom-call | tf_op jit(solution)/shard_map/reduce_blocks/pallas_call | solution.py:455
  98.7 1.0 copy.7

commit v5 on v4

--- a/solution.py
+++ b/solution.py
@@ -170,6 +170,16 @@
     to_y(L_PART, "L", 2, 0, own)
     over((0, LEN), "A", 0, 0, own)
 
+    for copy in small[1:]:
+        copy.wait()
+    loc = jnp.mod(columns_ref[...] - (b - 2) * ROWS, PANELS * ROWS)
+    slot = g * SLOTS + lax.broadcasted_iota(jnp.int32, (SLOTS, ROWS), 0)
+    live = slot < counts_ref[...].reshape(1, ROWS)
+    shard, within = loc // SHARD, loc % SHARD
+    row = shard * LEN + HEAD + within // 2 * BS
+    entry = (shard * 128 + within) * 2 + within % 2
+    code_ref[0:SLOTS, :] = jnp.where(live, row, HEAD)
+    code_ref[SLOTS:, :] = jnp.where(live, entry, SPAN * GROUP * 256)
     load_a.wait()
     turn(a_ref, turned, blocks, 0)
     got(("F", "x"))
@@ -248,16 +258,6 @@
     for copy in copies.values():
         copy.wait_send()
 
-    for copy in small[1:]:
-        copy.wait()
-    loc = jnp.mod(columns_ref[...] - (b - 2) * ROWS, PANELS * ROWS)
-    slot = g * SLOTS + lax.broadcasted_iota(jnp.int32, (SLOTS, ROWS), 0)
-    live = slot < counts_ref[...].reshape(1, ROWS)
-    shard, within = loc // SHARD, loc % SHARD
-    row = shard * LEN + HEAD + within // 2 * BS
-    entry = (shard * 128 + within) * 2 + within % 2
-    code_ref[0:SLOTS, :] = jnp.where(live, row, HEAD)
-    code_ref[SLOTS:, :] = jnp.where(live, entry, SPAN * GROUP * 256)
     for n in range(SPAN * GROUP):
         near = win_ref[n // GROUP, n % GROUP, 0:HEAD, :].astype(F32)[0:1].astype(jnp.int32)
         table_ref[n : n + 1, :] = (near + n // GROUP * CB) * (2 * CB)
@@ -340,10 +340,10 @@
         three, four = acc[4 * t + 2], acc[4 * t + 3]
         first = one + pltpu.roll(two, BS, 1)
         second = pltpu.roll(three, BS, 1) + four
-        place = t % GROUP * SPAN + t // GROUP
+        panel, row, columns = t // GROUP, t % GROUP // 2, t % 2
         block = jnp.where(low, first, second)
-        part_ref[place] = block
-        short_ref[place] = block.astype(BF16)
+        part_ref[columns, panel, row] = block
+        short_ref[columns, panel, row] = block.astype(BF16)
         return carry
 
     lax.fori_loop(0, BLOCKS, fold, 0, unroll=4)
@@ -355,8 +355,8 @@
     return pl.pallas_call(
         compute_kernel,
         out_shape=(
-            pltpu.VMEM((BLOCKS, BS, 2 * BS), F32),
-            pltpu.VMEM((BLOCKS, BS, 2 * BS), BF16),
+            pltpu.VMEM((2, SPAN, CB, BS, 2 * BS), F32),
+            pltpu.VMEM((2, SPAN, CB, BS, 2 * BS), BF16),
         ),
         in_specs=[smem, smem, vmem, vmem],
         out_specs=(vmem, vmem),
@@ -367,33 +367,45 @@
 
 
 def reduce_kernel(
-    part_ref, short_ref, out_ref, landed, landed_short, total, placed,
-    send_sem, recv_sem, send2, recv2,
+    part_ref, short_ref, out_ref, crossed, sums, landed, total, placed,
+    x_send, x_recv, y_send, y_recv, hop_send, hop_recv,
 ):
     b, g = lax.axis_index("blk"), lax.axis_index("grp")
+    y, h = g // 2, g % 2
+    mate = 1 - h
     others = [(g + n) % GROUP for n in range(1, GROUP)]
     barrier = pltpu.get_barrier_semaphore()
     for other in others:
         pl.semaphore_signal(barrier, inc=1, device_id=(b, other), device_id_type=MESH)
     pl.semaphore_wait(barrier, GROUP - 1)
-    first = []
-    for n, other in enumerate(others):
-        source, target = (part_ref, landed) if n % 2 else (short_ref, landed_short)
-        copy = pltpu.make_async_remote_copy(
-            src_ref=source.at[pl.ds(other * SPAN, SPAN)],
-            dst_ref=target.at[n // 2],
-            send_sem=send_sem.at[n],
-            recv_sem=recv_sem.at[n],
-            device_id=(b, other),
+
+    across = [
+        pltpu.make_async_remote_copy(
+            src_ref=short_ref.at[mate, d],
+            dst_ref=crossed.at[d],
+            send_sem=x_send.at[d],
+            recv_sem=x_recv.at[d],
+            device_id=(b, 2 * y + mate),
             device_id_type=MESH,
         )
+        for d in range(SPAN)
+    ]
+    for copy in across:
         copy.start()
-        first.append(copy)
     out_ref[...] = jnp.zeros(out_ref.shape, F32)
-    total[...] = part_ref[pl.ds(g * SPAN, SPAN)]
-    for n, copy in enumerate(first):
-        copy.wait_recv()
-        total[...] += (landed if n % 2 else landed_short)[n // 2].astype(F32)
+
+    def along(d):
+        return [
+            pltpu.make_async_remote_copy(
+                src_ref=sums.at[d, (y + n) % CB],
+                dst_ref=landed.at[d, n - 1],
+                send_sem=y_send.at[d, n - 1],
+                recv_sem=y_recv.at[d, n - 1],
+                device_id=(b, (g + 2 * n) % GROUP),
+                device_id_type=MESH,
+            )
+            for n in range(1, CB)
+        ]
 
     def hop(d):
         panel = (b + PANELS - 2 + d) % PANELS
@@ -401,23 +413,36 @@
         copy = pltpu.make_async_remote_copy(
             src_ref=total.at[d],
             dst_ref=placed.at[side, g],
-            send_sem=send2.at[d],
-            recv_sem=recv2.at[side],
+            send_sem=hop_send.at[d],
+            recv_sem=hop_recv.at[side],
             device_id=(b, owner),
             device_id_type=MESH,
         )
         return owner, side, copy
 
-    for d in range(SPAN):
-        owner, side, copy = hop(d)
-
-        @pl.when(owner != g)
-        def _(copy=copy):
-            copy.start()
-
-        @pl.when(owner == g)
-        def _(d=d, side=side):
-            placed[side, g] = total[d]
+    rows = [along(d) for d in range(SPAN)]
+    for step in range(SPAN + 1):
+        if step < SPAN:
+            across[step].wait_recv()
+            sums[step] = part_ref[h, step] + crossed[step].astype(F32)
+            for copy in rows[step]:
+                copy.start()
+        if step > 0:
+            d = step - 1
+            block = sums[d, y]
+            for n, copy in enumerate(rows[d]):
+                copy.wait_recv()
+                block += landed[d, n]
+            owner, side, copy = hop(d)
+            total[d] = block
+
+            @pl.when(owner != g)
+            def _(copy=copy):
+                copy.start()
+
+            @pl.when(owner == g)
+            def _(d=d, side=side):
+                placed[side, g] = total[d]
 
     for side in range(2):
         d = (2 * g + side + PANELS + 2 - b) % PANELS
@@ -428,8 +453,8 @@
             pltpu.make_async_remote_copy(
                 src_ref=rest,
                 dst_ref=rest,
-                send_sem=send2.at[0],
-                recv_sem=recv2.at[side],
+                send_sem=hop_send.at[0],
+                recv_sem=hop_recv.at[side],
                 device_id=(b, others[0]),
                 device_id_type=MESH,
             ).wait_recv()
@@ -446,26 +471,31 @@
         def _(copy=copy):
             copy.wait_send()
 
-    for copy in first:
-        copy.wait_send()
+        for copy in [across[d]] + rows[d]:
+            copy.wait_send()
 
 
 def reduced(part, short):
     vmem = pl.BlockSpec(memory_space=pltpu.VMEM)
+    block = (BS, 2 * BS)
+    dma = pltpu.SemaphoreType.DMA
     return pl.pallas_call(
         reduce_kernel,
         out_shape=jax.ShapeDtypeStruct((GROUP, CB, BS, BS), F32),
         in_specs=[vmem, vmem],
         out_specs=vmem,
         scratch_shapes=[
-            pltpu.VMEM((GROUP // 2 - 1, SPAN, BS, 2 * BS), F32),
-            pltpu.VMEM((GROUP // 2, SPAN, BS, 2 * BS), BF16),
-            pltpu.VMEM((SPAN, BS, 2 * BS), F32),
-            pltpu.VMEM((2, GROUP, BS, 2 * BS), F32),
-            pltpu.SemaphoreType.DMA((GROUP - 1,)),
-            pltpu.SemaphoreType.DMA((GROUP - 1,)),
-            pltpu.SemaphoreType.DMA((SPAN,)),
-            pltpu.SemaphoreType.DMA((2,)),
+            pltpu.VMEM((SPAN, CB, *block), BF16),
+            pltpu.VMEM((SPAN, CB, *block), F32),
+            pltpu.VMEM((SPAN, CB - 1, *block), F32),
+            pltpu.VMEM((SPAN, *block), F32),
+            pltpu.VMEM((2, GROUP, *block), F32),
+            dma((SPAN,)),
+            dma((SPAN,)),
+            dma((SPAN, CB - 1)),
+            dma((SPAN, CB - 1)),
+            dma((SPAN,)),
+            dma((2,)),
         ],
         compiler_params=pltpu.CompilerParams(
             collective_id=1, has_side_effects=True, vmem_limit_bytes=12 * 2**20

time: 101 us -> 102 us (level)
  Pallas kernels: 98.7 us -> 101 us
    pallas_call x1, Pallas kernels: 25.7 us -> 27.6 us  [reduced(): pl.pallas_call(reduce_kernel, out_shape=jax.ShapeDtypeStruct((GROUP, CB,...]
where the time goes in v5:
time: 102 us
  Pallas kernels  101 us (99%)
    pallas_call x1, Pallas kernels, gathered(): pl.pallas_call(gather_kernel, out_shape=(pltpu.VMEM((SPAN, GROUP, LEN, 2...  63.7 us
    pallas_call x1, Pallas kernels, reduced(): pl.pallas_call(reduce_kernel, out_shape=jax.ShapeDtypeStruct((GROUP, CB,...  27.6 us
    pallas_call x1, Pallas kernels, computed(): pl.pallas_call(compute_kernel, out_shape=(pltpu.VMEM((2, SPAN, CB, BS, 2...  9.19 us

profile of v5, /device:TPU:0, one launch (start us, length us, event | category | flops | bytes accessed | tf_op | source)
XLA Modules:
  0.0 101.5 jit_solution(13228192129488356157)
XLA Ops:
  0.0 63.7 %gather_window.1 = (bf16[5,8,1552,128]{3,2,1,0:T(8,128)(2,1)S(1)}, bf16[384,64,128]{2,1,0:T(8,128)(2,1)S(1)}, s32[4,384]{1,0:T(4,128)S(1)}, s32[56,128]{1,0:T(8,128)S(1)}) custom-call(bf16[48,64,64]{2,1,0:T(8,128)(2,1)} %p_ref.1, s32[48]{0:T(128)} %agg_hbm.1, s32[2,384]{1,0:T(2,128)} %bitcast.7, s32[384]{0:T(512)} %counts_hbm.1, bf16[2,64,64,384]{3,2,1,0:T(8,128)(2,1)} %bitcast.6), custom_call_target="tpu_custom_call" | custom-call | tf_op jit(solution)/shard_map/gather_window/pallas_call | solution.py:274
  63.8 9.2 %right_products.1 = (f32[2,5,4,64,128]{4,3,2,1,0:T(8,128)S(1)}, bf16[2,5,4,64,128]{4,3,2,1,0:T(8,128)(2,1)S(1)}) custom-call(s32[4,384]{1,0:T(4,128)S(1)} %get-tuple-element.11.code_ref, s32[7168]{0:T(1024)S(1)} %bitcast.5, bf16[62080,128]{1,0:T(8,128)(2,1)S(1)} %bitcast.4, bf16[384,64,128]{2,1,0:T(8,128)(2,1)S(1)} %get-tuple-element.14.blocks), custom_call_target="tpu_custom_call" | custom-call | tf_op jit(solution)/shard_map/right_products/pallas_call | solution.py:355
  73.0 27.6 %reduce_blocks.1 = f32[8,4,64,64]{3,2,1,0:T(8,128)S(1)} custom-call(f32[2,5,4,64,128]{4,3,2,1,0:T(8,128)S(1)} %get-tuple-element.15.part_ref, bf16[2,5,4,64,128]{4,3,2,1,0:T(8,128)(2,1)S(1)} %get-tuple-element.16.short_ref), custom_call_target="tpu_custom_call" | custom-call | tf_op jit(solution)/shard_map/reduce_blocks/pallas_call | solution.py:482
  100.5 1.0 copy.7

commit v6 on v4

--- a/solution.py
+++ b/solution.py
@@ -119,7 +119,7 @@
     keep.start()
     pl.semaphore_wait(barrier, len(greeted))
 
-    copies = {}
+    copies, arrived, settled = {}, [], set()
 
     def at(d, dy, dh):
         return win_ref.at[d, ((y + dy) % 4) * 2 + (h + dh) % 2]
@@ -142,6 +142,13 @@
     def got(*names):
         for name in names:
             copies[name].wait_recv()
+            arrived.append(name)
+
+    def settle():
+        for name in arrived:
+            if name not in settled:
+                settled.add(name)
+                copies[name].wait_send()
 
     def to_y(part, tag, d, dh, src=None):
         send((tag, "y+", d, dh), part, d, 0, dh, d, up_y, src)
@@ -170,6 +177,16 @@
     to_y(L_PART, "L", 2, 0, own)
     over((0, LEN), "A", 0, 0, own)
 
+    for copy in small[1:]:
+        copy.wait()
+    loc = jnp.mod(columns_ref[...] - (b - 2) * ROWS, PANELS * ROWS)
+    slot = g * SLOTS + lax.broadcasted_iota(jnp.int32, (SLOTS, ROWS), 0)
+    live = slot < counts_ref[...].reshape(1, ROWS)
+    shard, within = loc // SHARD, loc % SHARD
+    row = shard * LEN + HEAD + within // 2 * BS
+    entry = (shard * 128 + within) * 2 + within % 2
+    code_ref[0:SLOTS, :] = jnp.where(live, row, HEAD)
+    code_ref[SLOTS:, :] = jnp.where(live, entry, SPAN * GROUP * 256)
     load_a.wait()
     turn(a_ref, turned, blocks, 0)
     got(("F", "x"))
@@ -236,6 +253,7 @@
         over_far(L_PART, "L", dy, 1)
     for n, (dy, dh) in enumerate(((-1, 1), (1, 1), (2, 0), (2, 1))):
         left(win_ref, blocks, 4 + n)
+        settle()
         got(("F", "z+", dy, dh), ("F", "z-", dy, dh))
         over_far(F_PART, "F", dy, dh)
     for dh in (0, 1):
@@ -245,19 +263,10 @@
     for name in copies:
         if name[1] in ("s", "t"):
             got(name)
-    for copy in copies.values():
-        copy.wait_send()
-
-    for copy in small[1:]:
-        copy.wait()
-    loc = jnp.mod(columns_ref[...] - (b - 2) * ROWS, PANELS * ROWS)
-    slot = g * SLOTS + lax.broadcasted_iota(jnp.int32, (SLOTS, ROWS), 0)
-    live = slot < counts_ref[...].reshape(1, ROWS)
-    shard, within = loc // SHARD, loc % SHARD
-    row = shard * LEN + HEAD + within // 2 * BS
-    entry = (shard * 128 + within) * 2 + within % 2
-    code_ref[0:SLOTS, :] = jnp.where(live, row, HEAD)
-    code_ref[SLOTS:, :] = jnp.where(live, entry, SPAN * GROUP * 256)
+    for name in copies:
+        if name not in settled:
+            copies[name].wait_send()
+
     for n in range(SPAN * GROUP):
         near = win_ref[n // GROUP, n % GROUP, 0:HEAD, :].astype(F32)[0:1].astype(jnp.int32)
         table_ref[n : n + 1, :] = (near + n // GROUP * CB) * (2 * CB)
@@ -366,22 +375,27 @@
     )(codes, table, win, blocks)
 
 
+STEPS = ((2, 1, 1), (1, 1, 1), (3, 1, 1), (0, 1, 0), (2, 0, 1), (1, 0, 0), (3, 0, 0))
+
+
 def reduce_kernel(
     part_ref, short_ref, out_ref, landed, landed_short, total, placed,
     send_sem, recv_sem, send2, recv2,
 ):
     b, g = lax.axis_index("blk"), lax.axis_index("grp")
-    others = [(g + n) % GROUP for n in range(1, GROUP)]
+    y, h = g // 2, g % 2
+    others = [(y + dy) % CB * 2 + (h + dh) % 2 for dy, dh, _ in STEPS]
     barrier = pltpu.get_barrier_semaphore()
     for other in others:
         pl.semaphore_signal(barrier, inc=1, device_id=(b, other), device_id_type=MESH)
     pl.semaphore_wait(barrier, GROUP - 1)
-    first = []
-    for n, other in enumerate(others):
-        source, target = (part_ref, landed) if n % 2 else (short_ref, landed_short)
+    first, places = [], []
+    for n, (other, (dy, dh, short)) in enumerate(zip(others, STEPS)):
+        source, target = (short_ref, landed_short) if short else (part_ref, landed)
+        place = target.at[sum(step[2] == short for step in STEPS[:n])]
         copy = pltpu.make_async_remote_copy(
             src_ref=source.at[pl.ds(other * SPAN, SPAN)],
-            dst_ref=target.at[n // 2],
+            dst_ref=place,
             send_sem=send_sem.at[n],
             recv_sem=recv_sem.at[n],
             device_id=(b, other),
@@ -389,11 +403,12 @@
         )
         copy.start()
         first.append(copy)
+        places.append(place)
     out_ref[...] = jnp.zeros(out_ref.shape, F32)
     total[...] = part_ref[pl.ds(g * SPAN, SPAN)]
-    for n, copy in enumerate(first):
+    for copy, place in zip(first, places):
         copy.wait_recv()
-        total[...] += (landed if n % 2 else landed_short)[n // 2].astype(F32)
+        total[...] += place[...].astype(F32)
 
     def hop(d):
         panel = (b + PANELS - 2 + d) % PANELS

time: 101 us -> 98.3 us (0.973)
  Pallas kernels: 98.7 us -> 96.5 us
    pallas_call x1, Pallas kernels: 25.7 us -> 23.6 us  [reduced(): pl.pallas_call(reduce_kernel, out_shape=jax.ShapeDtypeStruct((GROUP, CB,...]
where the time goes in v6:
time: 98.3 us; the launch traced here: 97.5 us
  Pallas kernels  96.5 us (98%)
    pallas_call x1, Pallas kernels, gathered(): pl.pallas_call(gather_kernel, out_shape=(pltpu.VMEM((SPAN, GROUP, LEN, 2...  63.7 us
    pallas_call x1, Pallas kernels, reduced(): pl.pallas_call(reduce_kernel, out_shape=jax.ShapeDtypeStruct((GROUP, CB,...  23.6 us
    pallas_call x1, Pallas kernels, computed(): pl.pallas_call(compute_kernel, out_shape=(pltpu.VMEM((BLOCKS, BS, 2 * BS)...  9.19 us

profile of v6, /device:TPU:0, one launch (start us, length us, event | category | flops | bytes accessed | tf_op | source)
XLA Modules:
  0.0 97.5 jit_solution(2842349957623375692)
XLA Ops:
  0.0 63.7 %gather_window.1 = (bf16[5,8,1552,128]{3,2,1,0:T(8,128)(2,1)S(1)}, bf16[384,64,128]{2,1,0:T(8,128)(2,1)S(1)}, s32[4,384]{1,0:T(4,128)S(1)}, s32[56,128]{1,0:T(8,128)S(1)}) custom-call(bf16[48,64,64]{2,1,0:T(8,128)(2,1)} %p_ref.1, s32[48]{0:T(128)} %agg_hbm.1, s32[2,384]{1,0:T(2,128)} %bitcast.7, s32[384]{0:T(512)} %counts_hbm.1, bf16[2,64,64,384]{3,2,1,0:T(8,128)(2,1)} %bitcast.6), custom_call_target="tpu_custom_call" | custom-call | tf_op jit(solution)/shard_map/gather_window/pallas_call | solution.py:283
  63.8 9.2 %right_products.1 = (f32[40,64,128]{2,1,0:T(8,128)S(1)}, bf16[40,64,128]{2,1,0:T(8,128)(2,1)S(1)}) custom-call(s32[4,384]{1,0:T(4,128)S(1)} %get-tuple-element.11.code_ref, s32[7168]{0:T(1024)S(1)} %bitcast.5, bf16[62080,128]{1,0:T(8,128)(2,1)S(1)} %bitcast.4, bf16[384,64,128]{2,1,0:T(8,128)(2,1)S(1)} %get-tuple-element.14.blocks), custom_call_target="tpu_custom_call" | custom-call | tf_op jit(solution)/shard_map/right_products/pallas_call | solution.py:364
  73.0 23.6 %reduce_blocks.1 = f32[8,4,64,64]{3,2,1,0:T(8,128)S(1)} custom-call(f32[40,64,128]{2,1,0:T(8,128)S(1)} %get-tuple-element.15.part_ref, bf16[40,64,128]{2,1,0:T(8,128)(2,1)S(1)} %get-tuple-element.16.short_ref), custom_call_target="tpu_custom_call" | custom-call | tf_op jit(solution)/shard_map/reduce_blocks/pallas_call | solution.py:470
  96.5 1.0 copy.7

commit v7 on v6

--- a/solution.py
+++ b/solution.py
@@ -66,8 +66,8 @@
 
 def gather_kernel(
     p_ref, agg_hbm, columns_hbm, counts_hbm, a_hbm,
-    win_ref, blocks, code_ref, table_ref,
-    raw, own, a_ref, turned, agg_ref, columns_ref, counts_ref,
+    win_ref, blocks, code_ref, target_ref,
+    raw, own, a_ref, turned, agg_ref, columns_ref, counts_ref, shards, withins,
     local_sem, send_sem, recv_sem,
 ):
     b, g = lax.axis_index("blk"), lax.axis_index("grp")
@@ -183,10 +183,12 @@
     slot = g * SLOTS + lax.broadcasted_iota(jnp.int32, (SLOTS, ROWS), 0)
     live = slot < counts_ref[...].reshape(1, ROWS)
     shard, within = loc // SHARD, loc % SHARD
-    row = shard * LEN + HEAD + within // 2 * BS
-    entry = (shard * 128 + within) * 2 + within % 2
-    code_ref[0:SLOTS, :] = jnp.where(live, row, HEAD)
-    code_ref[SLOTS:, :] = jnp.where(live, entry, SPAN * GROUP * 256)
+    row = jnp.where(live, shard * LEN + HEAD + within // 2 * BS, HEAD)
+    shard = jnp.where(live, shard, SPAN * GROUP)
+    for value, target in ((row, code_ref), (shard, shards), (within, withins)):
+        target[...] = jnp.zeros((8, 128), jnp.int32)
+        for c in range(ROWS // 128):
+            target[2 * c : 2 * c + 2, :] = value[:, c * 128 : (c + 1) * 128]
     load_a.wait()
     turn(a_ref, turned, blocks, 0)
     got(("F", "x"))
@@ -267,12 +269,25 @@
         if name not in settled:
             copies[name].wait_send()
 
+    place = lax.broadcasted_iota(jnp.int32, (8, 128), 0) // 2 * 128
+    place += lax.broadcasted_iota(jnp.int32, (8, 128), 1)
+    shard, within = shards[...], withins[...]
+    target = jnp.full((8, 128), TARGETS, jnp.int32)
+    column = jnp.zeros((8, 128), jnp.int32)
+
+    def look(value, index):
+        table = jnp.broadcast_to(value, (8, 128))
+        return jnp.take_along_axis(table, index, axis=1, mode="promise_in_bounds")
+
     for n in range(SPAN * GROUP):
-        near = win_ref[n // GROUP, n % GROUP, 0:HEAD, :].astype(F32)[0:1].astype(jnp.int32)
-        table_ref[n : n + 1, :] = (near + n // GROUP * CB) * (2 * CB)
-        if n // GROUP == 2:
-            table_ref[n + 32 : n + 33, :] = near * 2
-    table_ref[SPAN * GROUP : 48, :] = jnp.full((8, 128), TARGETS, jnp.int32)
+        d = n // GROUP
+        near = win_ref[d, n % GROUP, 0:HEAD, :].astype(F32)[0:1].astype(jnp.int32)
+        found = look((near + d * CB) * (2 * CB), within)
+        target = jnp.where(shard == n, found, target)
+        if d == 2:
+            found = look(near * 2, place % SHARD)
+            column = jnp.where(place // SHARD == n % GROUP, found, column)
+    target_ref[...] = target + column + within % 2
 
 
 COPIES = 86 - 8
@@ -285,8 +300,8 @@
         out_shape=(
             pltpu.VMEM((SPAN, GROUP, LEN, 2 * BS), BF16),
             pltpu.VMEM((ROWS, BS, 2 * BS), BF16),
-            jax.ShapeDtypeStruct((2 * SLOTS, ROWS), jnp.int32),
-            jax.ShapeDtypeStruct((56, 128), jnp.int32),
+            jax.ShapeDtypeStruct((8, 128), jnp.int32),
+            jax.ShapeDtypeStruct((8, 128), jnp.int32),
         ),
         in_specs=[hbm] * 5,
         out_specs=(vmem, vmem, vmem, vmem),
@@ -298,6 +313,8 @@
             pltpu.VMEM((SHARD,), jnp.int32),
             pltpu.VMEM((SLOTS, ROWS), jnp.int32),
             pltpu.VMEM((ROWS,), jnp.int32),
+            pltpu.VMEM((8, 128), jnp.int32),
+            pltpu.VMEM((8, 128), jnp.int32),
             pltpu.SemaphoreType.DMA((6,)),
             pltpu.SemaphoreType.DMA((COPIES,)),
             pltpu.SemaphoreType.DMA((COPIES,)),
@@ -309,7 +326,7 @@
     )(*(pltpu.with_memory_space_constraint(x, pltpu.HBM) for x in (prolong, aggs, columns, counts, a)))
 
 
-def compute_kernel(code_ref, table_ref, win_ref, blocks, part_ref, short_ref, acc):
+def right_kernel(code_ref, target_ref, win_ref, blocks, acc):
     def clear(t, carry):
         acc[t] = jnp.zeros((BS, 2 * BS), F32)
         return carry
@@ -321,13 +338,12 @@
         def right(j, carry, shard=shard):
             i = shard * SHARD + j
             none = jnp.zeros((BS, 2 * BS), BF16)
-            column = table_ref[(48 + shard) * 128 + j]
             targets, picked = [], []
             for s in range(SLOTS):
-                row = pl.multiple_of(code_ref[s, i], HEAD)
-                entry = code_ref[SLOTS + s, i]
+                entry = i // 128 * 2 + s, i % 128
+                row = pl.multiple_of(code_ref[entry], HEAD)
                 picked.append(win_ref[pl.ds(row, BS), :])
-                targets.append(table_ref[entry // 2] + column + entry % 2)
+                targets.append(target_ref[entry])
             stack = jnp.concatenate(
                 [
                     jnp.concatenate([picked[0], none], axis=1),
@@ -342,6 +358,34 @@
 
         lax.fori_loop(0, SHARD, right, 0, unroll=SHARD)
 
+
+def multiplied(codes, targets, win, blocks):
+    smem = pl.BlockSpec(memory_space=pltpu.SMEM)
+    vmem = pl.BlockSpec(memory_space=pltpu.VMEM)
+    return pl.pallas_call(
+        right_kernel,
+        out_shape=pltpu.VMEM((ACCS, BS, 2 * BS), F32),
+        in_specs=[smem, smem, vmem, vmem],
+        out_specs=vmem,
+        compiler_params=pltpu.CompilerParams(vmem_limit_bytes=8 * 2**20),
+        name="right_products",
+    )(codes, targets, win, blocks)
+
+
+STEPS = ((2, 1, 1), (1, 1, 1), (3, 1, 1), (0, 1, 0), (2, 0, 1), (1, 0, 0), (3, 0, 0))
+
+
+def reduce_kernel(
+    acc, out_ref, part_ref, short_ref, landed, landed_short, total, placed,
+    send_sem, recv_sem, send2, recv2,
+):
+    b, g = lax.axis_index("blk"), lax.axis_index("grp")
+    y, h = g // 2, g % 2
+    others = [(y + dy) % CB * 2 + (h + dh) % 2 for dy, dh, _ in STEPS]
+    barrier = pltpu.get_barrier_semaphore()
+    for other in others:
+        pl.semaphore_signal(barrier, inc=1, device_id=(b, other), device_id_type=MESH)
+
     low = lax.broadcasted_iota(jnp.int32, (BS, 2 * BS), 1) < BS
 
     def fold(t, carry):
@@ -355,39 +399,7 @@
         short_ref[place] = block.astype(BF16)
         return carry
 
-    lax.fori_loop(0, BLOCKS, fold, 0, unroll=4)
-
-
-def computed(codes, table, win, blocks):
-    smem = pl.BlockSpec(memory_space=pltpu.SMEM)
-    vmem = pl.BlockSpec(memory_space=pltpu.VMEM)
-    return pl.pallas_call(
-        compute_kernel,
-        out_shape=(
-            pltpu.VMEM((BLOCKS, BS, 2 * BS), F32),
-            pltpu.VMEM((BLOCKS, BS, 2 * BS), BF16),
-        ),
-        in_specs=[smem, smem, vmem, vmem],
-        out_specs=(vmem, vmem),
-        scratch_shapes=[pltpu.VMEM((ACCS, BS, 2 * BS), F32)],
-        compiler_params=pltpu.CompilerParams(vmem_limit_bytes=16 * 2**20),
-        name="right_products",
-    )(codes, table, win, blocks)
-
-
-STEPS = ((2, 1, 1), (1, 1, 1), (3, 1, 1), (0, 1, 0), (2, 0, 1), (1, 0, 0), (3, 0, 0))
-
-
-def reduce_kernel(
-    part_ref, short_ref, out_ref, landed, landed_short, total, placed,
-    send_sem, recv_sem, send2, recv2,
-):
-    b, g = lax.axis_index("blk"), lax.axis_index("grp")
-    y, h = g // 2, g % 2
-    others = [(y + dy) % CB * 2 + (h + dh) % 2 for dy, dh, _ in STEPS]
-    barrier = pltpu.get_barrier_semaphore()
-    for other in others:
-        pl.semaphore_signal(barrier, inc=1, device_id=(b, other), device_id_type=MESH)
+    lax.fori_loop(0, BLOCKS, fold, 0, unroll=8)
     pl.semaphore_wait(barrier, GROUP - 1)
     first, places = [], []
     for n, (other, (dy, dh, short)) in enumerate(zip(others, STEPS)):
@@ -465,14 +477,16 @@
         copy.wait_send()
 
 
-def reduced(part, short):
+def reduced(acc):
     vmem = pl.BlockSpec(memory_space=pltpu.VMEM)
     return pl.pallas_call(
         reduce_kernel,
         out_shape=jax.ShapeDtypeStruct((GROUP, CB, BS, BS), F32),
-        in_specs=[vmem, vmem],
+        in_specs=[vmem],
         out_specs=vmem,
         scratch_shapes=[
+            pltpu.VMEM((BLOCKS, BS, 2 * BS), F32),
+            pltpu.VMEM((BLOCKS, BS, 2 * BS), BF16),
             pltpu.VMEM((GROUP // 2 - 1, SPAN, BS, 2 * BS), F32),
             pltpu.VMEM((GROUP // 2, SPAN, BS, 2 * BS), BF16),
             pltpu.VMEM((SPAN, BS, 2 * BS), F32),
@@ -486,11 +500,11 @@
             collective_id=1, has_side_effects=True, vmem_limit_bytes=12 * 2**20
         ),
         name="reduce_blocks",
-    )(part, short)
+    )(acc)
 
 
 def local(block_values, block_columns, row_counts, prolong_blocks, aggregates):
-    win, blocks, codes, table = gathered(
+    win, blocks, codes, targets = gathered(
         prolong_blocks,
         aggregates,
         block_columns.T,
@@ -498,7 +512,7 @@
         jnp.transpose(block_values, (1, 2, 3, 0)),
     )
     win = win.reshape(-1, 2 * BS)
-    return reduced(*computed(codes, table.reshape(-1), win, blocks))
+    return reduced(multiplied(codes, targets, win, blocks))
 
 
 def solution(mesh):

time: 98.3 us -> 95.8 us (0.975)
  Pallas kernels: 96.5 us -> 93.9 us
    pallas_call x1, Pallas kernels: 9.19 us -> 6.52 us  [multiplied(): pl.pallas_call(right_kernel, out_shape=pltpu.VMEM((ACCS, BS, 2 * BS), F32...]
where the time goes in v7:
time: 95.8 us; the launch traced here: 94.9 us
  Pallas kernels  93.9 us (98%)
  local copies, waits for them, and re-layouts  0.97 us (1%)
    pallas_call x1, Pallas kernels, gathered(): pl.pallas_call(gather_kernel, out_shape=(pltpu.VMEM((SPAN, GROUP, LEN, 2...  63.8 us
    pallas_call x1, Pallas kernels, reduced(): pl.pallas_call(reduce_kernel, out_shape=jax.ShapeDtypeStruct((GROUP, CB,...  23.6 us
    pallas_call x1, Pallas kernels, multiplied(): pl.pallas_call(right_kernel, out_shape=pltpu.VMEM((ACCS, BS, 2 * BS), F32...  6.52 us

profile of v7, /device:TPU:0, one launch (start us, length us, event | category | flops | bytes accessed | tf_op | source)
XLA Modules:
  0.0 94.9 jit_solution(11264962152988409751)
XLA Ops:
  0.0 63.8 %gather_window.1 = (bf16[5,8,1552,128]{3,2,1,0:T(8,128)(2,1)S(1)}, bf16[384,64,128]{2,1,0:T(8,128)(2,1)S(1)}, s32[8,128]{1,0:T(8,128)S(1)}, s32[8,128]{1,0:T(8,128)S(1)}) custom-call(bf16[48,64,64]{2,1,0:T(8,128)(2,1)} %p_ref.1, s32[48]{0:T(128)} %agg_hbm.1, s32[2,384]{1,0:T(2,128)} %bitcast.5, s32[384]{0:T(512)} %counts_hbm.1, bf16[2,64,64,384]{3,2,1,0:T(8,128)(2,1)} %bitcast.4), custom_call_target="tpu_custom_call" | custom-call | tf_op jit(solution)/shard_map/gather_window/pallas_call | solution.py:298
  63.9 6.5 %right_products.1.acc = f32[168,64,128]{2,1,0:T(8,128)S(1)} custom-call(s32[8,128]{1,0:T(8,128)S(1)} %get-tuple-element.9.code_ref, s32[8,128]{1,0:T(8,128)S(1)} %get-tuple-element.10.target_ref, bf16[62080,128]{1,0:T(8,128)(2,1)S(1)} %bitcast.3, bf16[384,64,128]{2,1,0:T(8,128)(2,1)S(1)} %get-tuple-element.12.blocks), custom_call_target="tpu_custom_call" | custom-call | tf_op jit(solution)/shard_map/right_products/pallas_call | solution.py:365
  70.4 23.6 %reduce_blocks.1 = f32[8,4,64,64]{3,2,1,0:T(8,128)S(1)} custom-call(f32[168,64,128]{2,1,0:T(8,128)S(1)} %right_products.1.acc), custom_call_target="tpu_custom_call" | custom-call | tf_op jit(solution)/shard_map/reduce_blocks/pallas_call | solution.py:482
  94.0 1.0 %copy.7 = f32[8,4,64,64]{3,2,1,0:T(8,128)} copy(f32[8,4,64,64]{3,2,1,0:T(8,128)S(1)} %reduce_blocks.1) | data formatting | bytes 1048576

commit v8 on v7

--- a/solution.py
+++ b/solution.py
@@ -49,7 +49,7 @@
     lax.fori_loop(0, 128, collect, 0, unroll=16)
 
 
-def left(win_ref, blocks, shard):
+def left(win_ref, blocks, lows, shard):
     def pair(j, carry):
         start = pl.multiple_of(HEAD + j * BS, HEAD)
         both = win_ref[2, shard, pl.ds(start, BS), :].T
@@ -58,7 +58,9 @@
             t = jnp.dot(
                 both[half * BS : (half + 1) * BS, :], blocks[i], preferred_element_type=F32
             )
-            blocks[i] = t.astype(BF16)
+            high = t.astype(BF16)
+            blocks[i] = high
+            lows[i] = (t - high.astype(F32)).astype(BF16)
         return carry
 
     lax.fori_loop(0, PAIRS, pair, 0, unroll=12)
@@ -66,7 +68,7 @@
 
 def gather_kernel(
     p_ref, agg_hbm, columns_hbm, counts_hbm, a_hbm,
-    win_ref, blocks, code_ref, target_ref,
+    win_ref, blocks, lows, code_ref, target_ref,
     raw, own, a_ref, turned, agg_ref, columns_ref, counts_ref, shards, withins,
     local_sem, send_sem, recv_sem,
 ):
@@ -241,20 +243,20 @@
     got(("L", "f+", 2, 1), ("L", "f-", 2, 1))
     over((0, LEN), "A", 2, 1)
     for shard in range(0, 2):
-        left(win_ref, blocks, shard)
+        left(win_ref, blocks, lows, shard)
     got(("F", "z+", 0, 1), ("F", "z-", 0, 1))
     over_far(F_PART, "F", 0, 1)
     for dy in (-1, 1):
         got(("F", "z+", dy, 0), ("F", "z-", dy, 0))
         over_far(F_PART, "F", dy, 0)
-        left(win_ref, blocks, 2 + (dy + 1) // 2)
+        left(win_ref, blocks, lows, 2 + (dy + 1) // 2)
     for d in (0, 4):
         got(("L", "y+", d, 1), ("L", "y-", d, 1))
         on_y(L_HALVES, "L", d, 1)
     for dy in (-1, 1):
         over_far(L_PART, "L", dy, 1)
     for n, (dy, dh) in enumerate(((-1, 1), (1, 1), (2, 0), (2, 1))):
-        left(win_ref, blocks, 4 + n)
+        left(win_ref, blocks, lows, 4 + n)
         settle()
         got(("F", "z+", dy, dh), ("F", "z-", dy, dh))
         over_far(F_PART, "F", dy, dh)
@@ -300,11 +302,12 @@
         out_shape=(
             pltpu.VMEM((SPAN, GROUP, LEN, 2 * BS), BF16),
             pltpu.VMEM((ROWS, BS, 2 * BS), BF16),
+            pltpu.VMEM((ROWS, BS, 2 * BS), BF16),
             jax.ShapeDtypeStruct((8, 128), jnp.int32),
             jax.ShapeDtypeStruct((8, 128), jnp.int32),
         ),
         in_specs=[hbm] * 5,
-        out_specs=(vmem, vmem, vmem, vmem),
+        out_specs=(vmem,) * 5,
         scratch_shapes=[
             pltpu.VMEM((SHARD, BS, BS), BF16),
             pltpu.VMEM((LEN, 2 * BS), BF16),
@@ -326,9 +329,10 @@
     )(*(pltpu.with_memory_space_constraint(x, pltpu.HBM) for x in (prolong, aggs, columns, counts, a)))
 
 
-def right_kernel(code_ref, target_ref, win_ref, blocks, acc):
+def right_kernel(code_ref, target_ref, win_ref, blocks, lows, acc_one, acc_two):
     def clear(t, carry):
-        acc[t] = jnp.zeros((BS, 2 * BS), F32)
+        acc_one[t] = jnp.zeros((BS, 2 * BS), F32)
+        acc_two[t] = jnp.zeros((BS, 2 * BS), F32)
         return carry
 
     lax.fori_loop(0, ACCS, clear, 0, unroll=8)
@@ -352,36 +356,37 @@
                 axis=0,
             )
             r = jnp.dot(blocks[i], stack, preferred_element_type=F32)
-            acc[targets[0]] += r[:, : 2 * BS]
-            acc[targets[1]] += r[:, 2 * BS :]
+            r += jnp.dot(lows[i], stack, preferred_element_type=F32)
+            acc_one[targets[0]] += r[:, : 2 * BS]
+            acc_two[targets[1]] += r[:, 2 * BS :]
             return carry
 
         lax.fori_loop(0, SHARD, right, 0, unroll=SHARD)
 
 
-def multiplied(codes, targets, win, blocks):
+def multiplied(codes, targets, win, blocks, lows):
     smem = pl.BlockSpec(memory_space=pltpu.SMEM)
     vmem = pl.BlockSpec(memory_space=pltpu.VMEM)
     return pl.pallas_call(
         right_kernel,
-        out_shape=pltpu.VMEM((ACCS, BS, 2 * BS), F32),
-        in_specs=[smem, smem, vmem, vmem],
-        out_specs=vmem,
+        out_shape=(pltpu.VMEM((ACCS, BS, 2 * BS), F32),) * SLOTS,
+        in_specs=[smem, smem, vmem, vmem, vmem],
+        out_specs=(vmem,) * SLOTS,
         compiler_params=pltpu.CompilerParams(vmem_limit_bytes=8 * 2**20),
         name="right_products",
-    )(codes, targets, win, blocks)
-
-
-STEPS = ((2, 1, 1), (1, 1, 1), (3, 1, 1), (0, 1, 0), (2, 0, 1), (1, 0, 0), (3, 0, 0))
+    )(codes, targets, win, blocks, lows)
+
+
+STEPS = ((2, 1), (1, 1), (3, 1), (0, 1), (2, 0), (1, 0), (3, 0))
 
 
 def reduce_kernel(
-    acc, out_ref, part_ref, short_ref, landed, landed_short, total, placed,
+    acc_one, acc_two, out_ref, part_ref, short_ref, landed, total, placed,
     send_sem, recv_sem, send2, recv2,
 ):
     b, g = lax.axis_index("blk"), lax.axis_index("grp")
     y, h = g // 2, g % 2
-    others = [(y + dy) % CB * 2 + (h + dh) % 2 for dy, dh, _ in STEPS]
+    others = [(y + dy) % CB * 2 + (h + dh) % 2 for dy, dh in STEPS]
     barrier = pltpu.get_barrier_semaphore()
     for other in others:
         pl.semaphore_signal(barrier, inc=1, device_id=(b, other), device_id_type=MESH)
@@ -389,8 +394,7 @@
     low = lax.broadcasted_iota(jnp.int32, (BS, 2 * BS), 1) < BS
 
     def fold(t, carry):
-        one, two = acc[4 * t], acc[4 * t + 1]
-        three, four = acc[4 * t + 2], acc[4 * t + 3]
+        one, two, three, four = (acc_one[4 * t + n] + acc_two[4 * t + n] for n in range(4))
         first = one + pltpu.roll(two, BS, 1)
         second = pltpu.roll(three, BS, 1) + four
         place = t % GROUP * SPAN + t // GROUP
@@ -401,13 +405,11 @@
 
     lax.fori_loop(0, BLOCKS, fold, 0, unroll=8)
     pl.semaphore_wait(barrier, GROUP - 1)
-    first, places = [], []
-    for n, (other, (dy, dh, short)) in enumerate(zip(others, STEPS)):
-        source, target = (short_ref, landed_short) if short else (part_ref, landed)
-        place = target.at[sum(step[2] == short for step in STEPS[:n])]
+    first = []
+    for n, other in enumerate(others):
         copy = pltpu.make_async_remote_copy(
-            src_ref=source.at[pl.ds(other * SPAN, SPAN)],
-            dst_ref=place,
+            src_ref=short_ref.at[pl.ds(other * SPAN, SPAN)],
+            dst_ref=landed.at[n],
             send_sem=send_sem.at[n],
             recv_sem=recv_sem.at[n],
             device_id=(b, other),
@@ -415,12 +417,11 @@
         )
         copy.start()
         first.append(copy)
-        places.append(place)
     out_ref[...] = jnp.zeros(out_ref.shape, F32)
     total[...] = part_ref[pl.ds(g * SPAN, SPAN)]
-    for copy, place in zip(first, places):
+    for n, copy in enumerate(first):
         copy.wait_recv()
-        total[...] += place[...].astype(F32)
+        total[...] += landed[n].astype(F32)
 
     def hop(d):
         panel = (b + PANELS - 2 + d) % PANELS
@@ -477,18 +478,17 @@
         copy.wait_send()
 
 
-def reduced(acc):
+def reduced(acc_one, acc_two):
     vmem = pl.BlockSpec(memory_space=pltpu.VMEM)
     return pl.pallas_call(
         reduce_kernel,
         out_shape=jax.ShapeDtypeStruct((GROUP, CB, BS, BS), F32),
-        in_specs=[vmem],
+        in_specs=[vmem, vmem],
         out_specs=vmem,
         scratch_shapes=[
             pltpu.VMEM((BLOCKS, BS, 2 * BS), F32),
             pltpu.VMEM((BLOCKS, BS, 2 * BS), BF16),
-            pltpu.VMEM((GROUP // 2 - 1, SPAN, BS, 2 * BS), F32),
-            pltpu.VMEM((GROUP // 2, SPAN, BS, 2 * BS), BF16),
+            pltpu.VMEM((GROUP - 1, SPAN, BS, 2 * BS), BF16),
             pltpu.VMEM((SPAN, BS, 2 * BS), F32),
             pltpu.VMEM((2, GROUP, BS, 2 * BS), F32),
             pltpu.SemaphoreType.DMA((GROUP - 1,)),
@@ -500,11 +500,11 @@
             collective_id=1, has_side_effects=True, vmem_limit_bytes=12 * 2**20
         ),
         name="reduce_blocks",
-    )(acc)
+    )(acc_one, acc_two)
 
 
 def local(block_values, block_columns, row_counts, prolong_blocks, aggregates):
-    win, blocks, codes, targets = gathered(
+    win, blocks, lows, codes, targets = gathered(
         prolong_blocks,
         aggregates,
         block_columns.T,
@@ -512,7 +512,7 @@
         jnp.transpose(block_values, (1, 2, 3, 0)),
     )
     win = win.reshape(-1, 2 * BS)
-    return reduced(multiplied(codes, targets, win, blocks))
+    return reduced(*multiplied(codes, targets, win, blocks, lows))
 
 
 def solution(mesh):

time: 95.8 us -> 96.1 us (level)
    pallas_call x1, Pallas kernels: 6.52 us -> 8.43 us  [multiplied(): pl.pallas_call(right_kernel, out_shape=(pltpu.VMEM((ACCS, BS, 2 * BS), F3...]
    pallas_call x1, Pallas kernels: 23.6 us -> 21.8 us  [reduced(): pl.pallas_call(reduce_kernel, out_shape=jax.ShapeDtypeStruct((GROUP, CB,...]
where the time goes in v8:
time: 96.1 us; the launch traced here: 95.1 us
  Pallas kernels  94.1 us (98%)
  local copies, waits for them, and re-layouts  0.97 us (1%)
    pallas_call x1, Pallas kernels, gathered(): pl.pallas_call(gather_kernel, out_shape=(pltpu.VMEM((SPAN, GROUP, LEN, 2...  63.9 us
    pallas_call x1, Pallas kernels, reduced(): pl.pallas_call(reduce_kernel, out_shape=jax.ShapeDtypeStruct((GROUP, CB,...  21.8 us
    pallas_call x1, Pallas kernels, multiplied(): pl.pallas_call(right_kernel, out_shape=(pltpu.VMEM((ACCS, BS, 2 * BS), F3...  8.43 us

profile of v8, /device:TPU:0, one launch (start us, length us, event | category | flops | bytes accessed | tf_op | source)
XLA Modules:
  0.0 95.1 jit_solution(17260203508237073569)
XLA Ops:
  0.0 63.9 %gather_window.1 = (bf16[5,8,1552,128]{3,2,1,0:T(8,128)(2,1)S(1)}, bf16[384,64,128]{2,1,0:T(8,128)(2,1)S(1)}, bf16[384,64,128]{2,1,0:T(8,128)(2,1)S(1)}, s32[8,128]{1,0:T(8,128)S(1)}, s32[8,128]{1,0:T(8,128)S(1)}) custom-call(bf16[48,64,64]{2,1,0:T(8,128)(2,1)} %p_ref.1, s32[48]{0:T(128)} %agg_hbm.1, s32[2,384]{1,0:T(2,128)} %bitcast.5, s32[384]{0:T(512)} %counts_hbm.1, ...), custom_call_target="tpu_custom_call" | custom-call | tf_op jit(solution)/shard_map/gather_window/pallas_call | solution.py:300
  63.9 8.4 %right_products.1 = (f32[168,64,128]{2,1,0:T(8,128)S(1)}, f32[168,64,128]{2,1,0:T(8,128)S(1)}) custom-call(s32[8,128]{1,0:T(8,128)S(1)} %get-tuple-element.12.code_ref, s32[8,128]{1,0:T(8,128)S(1)} %get-tuple-element.13.target_ref, bf16[62080,128]{1,0:T(8,128)(2,1)S(1)} %bitcast.3, bf16[384,64,128]{2,1,0:T(8,128)(2,1)S(1)} %get-tuple-element.15.blocks, ...), custom_call_target="tpu_custom_call" | custom-call | tf_op jit(solution)/shard_map/right_products/pallas_call | solution.py:370
  72.3 21.8 %reduce_blocks.1 = f32[8,4,64,64]{3,2,1,0:T(8,128)S(1)} custom-call(f32[168,64,128]{2,1,0:T(8,128)S(1)} %get-tuple-element.17.acc_one, f32[168,64,128]{2,1,0:T(8,128)S(1)} %get-tuple-element.18.acc_two), custom_call_target="tpu_custom_call" | custom-call | tf_op jit(solution)/shard_map/reduce_blocks/pallas_call | solution.py:483
  94.2 1.0 %copy.7 = f32[8,4,64,64]{3,2,1,0:T(8,128)} copy(f32[8,4,64,64]{3,2,1,0:T(8,128)S(1)} %reduce_blocks.1) | data formatting | bytes 1048576

commit v9 on v7

--- a/solution.py
+++ b/solution.py
@@ -326,9 +326,10 @@
     )(*(pltpu.with_memory_space_constraint(x, pltpu.HBM) for x in (prolong, aggs, columns, counts, a)))
 
 
-def right_kernel(code_ref, target_ref, win_ref, blocks, acc):
+def right_kernel(code_ref, target_ref, win_ref, blocks, acc_one, acc_two):
     def clear(t, carry):
-        acc[t] = jnp.zeros((BS, 2 * BS), F32)
+        acc_one[t] = jnp.zeros((BS, 2 * BS), F32)
+        acc_two[t] = jnp.zeros((BS, 2 * BS), F32)
         return carry
 
     lax.fori_loop(0, ACCS, clear, 0, unroll=8)
@@ -352,8 +353,8 @@
                 axis=0,
             )
             r = jnp.dot(blocks[i], stack, preferred_element_type=F32)
-            acc[targets[0]] += r[:, : 2 * BS]
-            acc[targets[1]] += r[:, 2 * BS :]
+            acc_one[targets[0]] += r[:, : 2 * BS]
+            acc_two[targets[1]] += r[:, 2 * BS :]
             return carry
 
         lax.fori_loop(0, SHARD, right, 0, unroll=SHARD)
@@ -364,9 +365,9 @@
     vmem = pl.BlockSpec(memory_space=pltpu.VMEM)
     return pl.pallas_call(
         right_kernel,
-        out_shape=pltpu.VMEM((ACCS, BS, 2 * BS), F32),
+        out_shape=(pltpu.VMEM((ACCS, BS, 2 * BS), F32),) * SLOTS,
         in_specs=[smem, smem, vmem, vmem],
-        out_specs=vmem,
+        out_specs=(vmem,) * SLOTS,
         compiler_params=pltpu.CompilerParams(vmem_limit_bytes=8 * 2**20),
         name="right_products",
     )(codes, targets, win, blocks)
@@ -376,7 +377,7 @@
 
 
 def reduce_kernel(
-    acc, out_ref, part_ref, short_ref, landed, landed_short, total, placed,
+    acc_one, acc_two, out_ref, part_ref, short_ref, landed, landed_short, total, placed,
     send_sem, recv_sem, send2, recv2,
 ):
     b, g = lax.axis_index("blk"), lax.axis_index("grp")
@@ -389,8 +390,7 @@
     low = lax.broadcasted_iota(jnp.int32, (BS, 2 * BS), 1) < BS
 
     def fold(t, carry):
-        one, two = acc[4 * t], acc[4 * t + 1]
-        three, four = acc[4 * t + 2], acc[4 * t + 3]
+        one, two, three, four = (acc_one[4 * t + n] + acc_two[4 * t + n] for n in range(4))
         first = one + pltpu.roll(two, BS, 1)
         second = pltpu.roll(three, BS, 1) + four
         place = t % GROUP * SPAN + t // GROUP
@@ -477,12 +477,12 @@
         copy.wait_send()
 
 
-def reduced(acc):
+def reduced(acc_one, acc_two):
     vmem = pl.BlockSpec(memory_space=pltpu.VMEM)
     return pl.pallas_call(
         reduce_kernel,
         out_shape=jax.ShapeDtypeStruct((GROUP, CB, BS, BS), F32),
-        in_specs=[vmem],
+        in_specs=[vmem, vmem],
         out_specs=vmem,
         scratch_shapes=[
             pltpu.VMEM((BLOCKS, BS, 2 * BS), F32),
@@ -500,7 +500,7 @@
             collective_id=1, has_side_effects=True, vmem_limit_bytes=12 * 2**20
         ),
         name="reduce_blocks",
-    )(acc)
+    )(acc_one, acc_two)
 
 
 def local(block_values, block_columns, row_counts, prolong_blocks, aggregates):
@@ -512,7 +512,7 @@
         jnp.transpose(block_values, (1, 2, 3, 0)),
     )
     win = win.reshape(-1, 2 * BS)
-    return reduced(multiplied(codes, targets, win, blocks))
+    return reduced(*multiplied(codes, targets, win, blocks))
 
 
 def solution(mesh):

time: 95.8 us -> 94.6 us (0.987)
  Pallas kernels: 93.9 us -> 92.7 us
    pallas_call x1, Pallas kernels: 6.52 us -> 5.21 us  [multiplied(): pl.pallas_call(right_kernel, out_shape=(pltpu.VMEM((ACCS, BS, 2 * BS), F3...]
where the time goes in v9:
time: 94.6 us; the launch traced here: 93.7 us
  Pallas kernels  92.7 us (98%)
  local copies, waits for them, and re-layouts  0.97 us (1%)
    pallas_call x1, Pallas kernels, gathered(): pl.pallas_call(gather_kernel, out_shape=(pltpu.VMEM((SPAN, GROUP, LEN, 2...  63.9 us
    pallas_call x1, Pallas kernels, reduced(): pl.pallas_call(reduce_kernel, out_shape=jax.ShapeDtypeStruct((GROUP, CB,...  23.6 us
    pallas_call x1, Pallas kernels, multiplied(): pl.pallas_call(right_kernel, out_shape=(pltpu.VMEM((ACCS, BS, 2 * BS), F3...  5.21 us

profile of v9, /device:TPU:0, one launch (start us, length us, event | category | flops | bytes accessed | tf_op | source)
XLA Modules:
  0.0 93.7 jit_solution(10510378761936397464)
XLA Ops:
  0.0 63.9 %gather_window.1 = (bf16[5,8,1552,128]{3,2,1,0:T(8,128)(2,1)S(1)}, bf16[384,64,128]{2,1,0:T(8,128)(2,1)S(1)}, s32[8,128]{1,0:T(8,128)S(1)}, s32[8,128]{1,0:T(8,128)S(1)}) custom-call(bf16[48,64,64]{2,1,0:T(8,128)(2,1)} %p_ref.1, s32[48]{0:T(128)} %agg_hbm.1, s32[2,384]{1,0:T(2,128)} %bitcast.5, s32[384]{0:T(512)} %counts_hbm.1, bf16[2,64,64,384]{3,2,1,0:T(8,128)(2,1)} %bitcast.4), custom_call_target="tpu_custom_call" | custom-call | tf_op jit(solution)/shard_map/gather_window/pallas_call | solution.py:298
  63.9 5.2 %right_products.1 = (f32[168,64,128]{2,1,0:T(8,128)S(1)}, f32[168,64,128]{2,1,0:T(8,128)S(1)}) custom-call(s32[8,128]{1,0:T(8,128)S(1)} %get-tuple-element.11.code_ref, s32[8,128]{1,0:T(8,128)S(1)} %get-tuple-element.12.target_ref, bf16[62080,128]{1,0:T(8,128)(2,1)S(1)} %bitcast.3, bf16[384,64,128]{2,1,0:T(8,128)(2,1)S(1)} %get-tuple-element.14.blocks), custom_call_target="tpu_custom_call" | custom-call | tf_op jit(solution)/shard_map/right_products/pallas_call | solution.py:366
  69.1 23.6 %reduce_blocks.1 = f32[8,4,64,64]{3,2,1,0:T(8,128)S(1)} custom-call(f32[168,64,128]{2,1,0:T(8,128)S(1)} %get-tuple-element.15.acc_one, f32[168,64,128]{2,1,0:T(8,128)S(1)} %get-tuple-element.16.acc_two), custom_call_target="tpu_custom_call" | custom-call | tf_op jit(solution)/shard_map/reduce_blocks/pallas_call | solution.py:482
  92.7 1.0 %copy.7 = f32[8,4,64,64]{3,2,1,0:T(8,128)} copy(f32[8,4,64,64]{3,2,1,0:T(8,128)S(1)} %reduce_blocks.1) | data formatting | bytes 1048576
